TPU v7x, 768 devices: a whole 4x8x12 slice. The times are simulated.
768 devices in a mesh: dp: 12 (over z), node: 8 (over x, core), local: 8 (over y).
Axes of the slice: x: 4, y: 8, z: 12, core: 2. Of those that a mesh axis runs over, the one named last changes fastest.
Arguments:
- tokens: bfloat16 [98304, 2048], P(('dp', 'node', 'local')), may hold values from -6 to 6
- expert_ids: int32 [98304, 1], P(('dp', 'node', 'local')), may hold values from 0 to 63; in each aligned block of 128 rows (0 to 127, 128 to 255, ...) at most 4 rows name the same one
- gates: float32 [98304, 1], P(('dp', 'node', 'local')), may hold values from 0.05 to 1
- out_grad: bfloat16 [98304, 2048], P(('dp', 'node', 'local')), may hold values from -1.1953125 to 1.1953125
- w_gate: bfloat16 [64, 2048, 384], P(('node', 'local')), may hold values from -0.125 to 0.125
- w_up: bfloat16 [64, 2048, 384], P(('node', 'local')), may hold values from -0.125 to 0.125
- w_down: bfloat16 [64, 384, 2048], P(('node', 'local')), may hold values from -0.3125 to 0.3125
Outputs:
- layer_out: bfloat16 [98304, 2048], P(('dp', 'node', 'local'))
- grad_in: bfloat16 [98304, 2048], P(('dp', 'node', 'local'))
- grad_gates: float32 [98304, 1], P(('dp', 'node', 'local'))
- grad_w_gate: bfloat16 [64, 384, 2048], P(('node', 'local'), 'dp')
- grad_w_up: bfloat16 [64, 384, 2048], P(('node', 'local'), 'dp')
- grad_w_down: bfloat16 [64, 384, 2048], P(('node', 'local'), 'dp')
Inputs may be any that keep to these rules, and one draw needn't show every extreme that they name: `expert_ids`: each token names one expert; among the tokens of one device no expert is named more than 4 times, and in some device one expert is named exactly 4 times; every expert is named somewhere.
All inputs are finite; a program needn't handle non-finite values.
Results may differ from a plain program's by a relative error of at most 0.02.
Values may be sent and summed in bfloat16 or wider, within the bound.
No kernel may reach another device: no remote copies, remote signals or barrier semaphores. Data moves between devices by JAX's collectives and lax.ppermute only.
A program may use at most 64 MiB of HBM per device.

v0:
```python
import jax
import jax.numpy as jnp
from jax import lax
from jax.sharding import PartitionSpec as P


def silu_parts(pre_gate):
    sigma = jax.nn.sigmoid(pre_gate)
    return (pre_gate * sigma, sigma * (1.0 + pre_gate * (1.0 - sigma)))


def move_rows(buffer):
    return lax.all_to_all(buffer, ("node", "local"), split_axis=0, concat_axis=0, tiled=True)


def contract_rows(factor, operand):
    return lax.dot_general(
        factor, operand, (((0,), (0,)), ((), ())), preferred_element_type=jnp.float32
    )


def contract_cols(factor, operand):
    return lax.dot_general(
        factor, operand, (((1,), (1,)), ((), ())), preferred_element_type=jnp.float32
    )


def on_device(tokens, expert_ids, gates, out_grad, w_gate, w_up, w_down):
    nodes = lax.axis_size("node")
    experts = nodes * lax.axis_size("local")
    tok_rows, width = tokens.shape
    topk = expert_ids.shape[1]
    capacity = max(2, 2 * tok_rows * topk // experts)
    assigned = tok_rows * topk
    flat_ids = expert_ids.reshape(assigned)
    onehot = (flat_ids[:, None] == jnp.arange(experts, dtype=jnp.int32)[None, :]).astype(jnp.int32)
    rank = jnp.cumsum(onehot, axis=0) - onehot
    target = flat_ids * capacity + jnp.sum(rank * onehot, axis=1)
    anchor = (
        jnp.full((experts * capacity,), assigned, jnp.int32)
        .at[target]
        .set(jnp.arange(assigned, dtype=jnp.int32))
    )
    live = anchor < assigned
    clipped = jnp.minimum(anchor, assigned - 1)
    token_of = clipped // topk
    outgoing = jnp.where(live[:, None], tokens[token_of], jnp.zeros((), tokens.dtype))
    grad_wide = out_grad.astype(jnp.float32)
    scaled = (
        (gates[:, :, None] * grad_wide[:, None, :]).astype(jnp.bfloat16).reshape(assigned, width)
    )
    outgoing_grad = jnp.where(live[:, None], scaled[clipped], jnp.zeros((), jnp.bfloat16))
    incoming = move_rows(outgoing)
    pre_gate = jnp.dot(incoming, w_gate[0], preferred_element_type=jnp.float32)
    pre_up = jnp.dot(incoming, w_up[0], preferred_element_type=jnp.float32)
    activated, slope = silu_parts(pre_gate)
    hidden = (activated * pre_up).astype(jnp.bfloat16)
    expert_out = jnp.dot(hidden, w_down[0], preferred_element_type=jnp.float32).astype(jnp.bfloat16)
    returned = move_rows(expert_out)
    expert_grad = move_rows(outgoing_grad)
    grad_hidden = contract_cols(expert_grad, w_down[0])
    grad_pre_gate = (grad_hidden * pre_up * slope).astype(jnp.bfloat16)
    grad_pre_up = (grad_hidden * activated).astype(jnp.bfloat16)
    input_grad = (
        contract_cols(grad_pre_gate, w_gate[0]) + contract_cols(grad_pre_up, w_up[0])
    ).astype(jnp.bfloat16)
    returned_grad = move_rows(input_grad)
    slot_out = returned[target].reshape(tok_rows, topk, width).astype(jnp.float32)
    layer_out = jnp.sum(gates[:, :, None] * slot_out, axis=1).astype(jnp.bfloat16)
    grad_gates = jnp.sum(grad_wide[:, None, :] * slot_out, axis=2)
    grad_in = jnp.sum(
        returned_grad[target].reshape(tok_rows, topk, width).astype(jnp.float32), axis=1
    ).astype(jnp.bfloat16)
    pieces = []
    for factor, operand in (
        (grad_pre_gate, incoming),
        (grad_pre_up, incoming),
        (hidden, expert_grad),
    ):
        pieces.append(contract_rows(factor, operand))
    shares = lax.psum_scatter(
        jnp.stack(pieces, axis=1).astype(jnp.bfloat16), "dp", scatter_dimension=0, tiled=True
    ).astype(jnp.float32)
    grad_w_gate = shares[None, :, 0, :].astype(jnp.bfloat16)
    grad_w_up = shares[None, :, 1, :].astype(jnp.bfloat16)
    grad_w_down = shares[None, :, 2, :].astype(jnp.bfloat16)
    return (layer_out, grad_in, grad_gates, grad_w_gate, grad_w_up, grad_w_down)


def solution(mesh):
    return jax.shard_map(
        on_device,
        mesh=mesh,
        in_specs=(
            P(("dp", "node", "local"), None),
            P(("dp", "node", "local"), None),
            P(("dp", "node", "local"), None),
            P(("dp", "node", "local"), None),
            P(("node", "local"), None, None),
            P(("node", "local"), None, None),
            P(("node", "local"), None, None),
        ),
        out_specs=(
            P(("dp", "node", "local"), None),
            P(("dp", "node", "local"), None),
            P(("dp", "node", "local"), None),
            P(("node", "local"), "dp", None),
            P(("node", "local"), "dp", None),
            P(("node", "local"), "dp", None),
        ),
        check_vma=False,
    )
```

profile of v0, /device:TPU:6, one launch (start us, length us, event | category | flops | bytes accessed | tf_op | source)
XLA Modules:
  0.0 195.1 jit_solution(4554199952669803379)
XLA Ops:
  7.2 0.9 fusion.18
  9.7 1.0 scatter_custom_fusion
  10.7 1.2 fusion.15
  11.9 1.4 gather_fusion.2
  13.3 1.2 gather.20
  14.6 1.4 gather_fusion
  15.9 1.2 gather.17
  17.3 3.6 %broadcast_select_fusion = (bf16[64,4,2048]{2,1,0:T(4,128)(2,1)}, bf16[64,4,2048]{2,1,0:T(4,128)(2,1)S(1)}) fusion(bf16[64,4,2048]{2,1,0:T(4,128)(2,1)} %gather.20, pred[64,4]{1,0:T(8,128)(4,1)S(1)} %broadcast_in_dim.32, bf16[64,4,2048]{2,1,0:T(4,128)(2,1)} %gather.17), kind=kLoop, calls=%fused_computation.31 | loop fusion | flops 1048576 | bytes 4194560 | tf_op jit(solution)/shard_map/jit(_where)/select_n | solution.py:52
  20.9 41.0 %all_to_all.42 = bf16[64,4,2048]{2,1,0:T(4,128)(2,1)} all-to-all(bf16[64,4,2048]{2,1,0:T(4,128)(2,1)S(1)} %get-tuple-element.15), channel_id=1, replica_groups=mesh['dp'=12,'node'=8,'local'=8] {'node','local'}, dimensions={0} | all-to-all | bytes 2097152 | tf_op jit(solution)/shard_map/all_to_all | solution.py:13
  61.9 7.8 %all-to-all-start.2 = ((bf16[64,4,2048]{2,1,0:T(4,128)(2,1)}), bf16[64,4,2048]{2,1,0:T(4,128)(2,1)}, u32[]{:S(2)}, u32[]{:S(2)}) async-start(bf16[64,4,2048]{2,1,0:T(4,128)(2,1)} %get-tuple-element.14), calls=%async_computation.2 | async-start | bytes 2097152 | tf_op jit(solution)/shard_map/all_to_all | solution.py:13
  69.8 1.3 all_to_all.29
  71.1 3.0 %fusion.12 = f32[256,384]{1,0:T(8,128)} fusion(bf16[256,2048]{1,0:T(8,128)(2,1)S(1)} %all_to_all.29, bf16[1,2048,384]{2,1,0:T(8,128)(2,1)} %param.11), kind=kOutput, calls=%fused_computation.23 | convolution fusion | flops 402653184 | bytes 3014656 | tf_op jit(solution)/shard_map/dot_general | solution.py:54
  74.1 1.5 fusion.8
  75.6 21.4 %all-to-all-done.2 = bf16[64,4,2048]{2,1,0:T(4,128)(2,1)} async-done(((bf16[64,4,2048]{2,1,0:T(4,128)(2,1)}), bf16[64,4,2048]{2,1,0:T(4,128)(2,1)}, u32[]{:S(2)}, u32[]{:S(2)}) %all-to-all-start.2) | async-done | bytes 1048608 | tf_op jit(solution)/shard_map/all_to_all | solution.py:13
  97.0 2.2 %all_to_all.34 = bf16[256,2048]{1,0:T(8,128)(2,1)} reshape(bf16[64,4,2048]{2,1,0:T(4,128)(2,1)} %all-to-all-done.2) | data formatting | bytes 2097152 | tf_op jit(solution)/shard_map/all_to_all | solution.py:13
  99.2 2.2 %multiply_convert_fusion = (bf16[256,384]{1,0:T(8,128)(2,1)S(1)}, bf16[256,384]{1,0:T(8,128)(2,1)S(1)}, bf16[256,384]{1,0:T(8,128)(2,1)S(1)}) fusion(f32[256,384]{1,0:T(8,128)} %fusion.12, f32[256,384]{1,0:T(8,128)} %fusion.8, bf16[256,2048]{1,0:T(8,128)(2,1)} %all_to_all.34, bf16[1,384,2048]{2,1,0:T(8,128)(2,1)S(1)} %copy-done), kind=kOutput, calls=%fused_computation.33 | convolution fusion | flops 404127744 | bytes 3997696 | tf_op jit(solution)/shard_map/dot_general | solution.py:23
  103.9 2.4 %pad_maximum_fusion = bf16[384,3,2048]{2,0,1:T(8,128)(2,1)} fusion(bf16[384,1,2048]{2,0,1:T(8,128)(2,1)S(1)} %fusion.2, bf16[384,1,2048]{2,0,1:T(8,128)(2,1)S(1)} %fusion.1, bf16[384,1,2048]{2,0,1:T(8,128)(2,1)S(1)} %fusion), kind=kLoop, calls=%fused_computation.5 | loop fusion | flops 4718592 | bytes 9437184 | tf_op jit(solution)/shard_map/stack | solution.py:82
  106.3 1.4 copy-done.2
  107.7 1.8 fusion.10
  110.3 1.2 all_to_all.35
  111.5 7.7 %all-to-all-start.3 = ((bf16[64,4,2048]{2,1,0:T(4,128)(2,1)}), bf16[64,4,2048]{2,1,0:T(4,128)(2,1)S(1)}, u32[]{:S(2)}, u32[]{:S(2)}) async-start(bf16[64,4,2048]{2,1,0:T(4,128)(2,1)} %all_to_all.35), calls=%async_computation.3 | async-start | bytes 2097152 | tf_op jit(solution)/shard_map/all_to_all | solution.py:13
  119.2 1.7 convolution_convert_fusion.3
  120.9 2.3 %all_to_all.30 = bf16[64,4,2048]{2,1,0:T(4,128)(2,1)} reshape(bf16[256,2048]{1,0:T(8,128)(2,1)} %convolution_convert_fusion.3) | data formatting | bytes 2097152 | tf_op jit(solution)/shard_map/all_to_all | solution.py:13
  123.2 23.4 %all-to-all-done.3 = bf16[64,4,2048]{2,1,0:T(4,128)(2,1)S(1)} async-done(((bf16[64,4,2048]{2,1,0:T(4,128)(2,1)}), bf16[64,4,2048]{2,1,0:T(4,128)(2,1)S(1)}, u32[]{:S(2)}, u32[]{:S(2)}) %all-to-all-start.3) | async-done | bytes 1048608 | tf_op jit(solution)/shard_map/all_to_all | solution.py:13
  146.6 7.7 %all-to-all-start.1 = ((bf16[64,4,2048]{2,1,0:T(4,128)(2,1)}), bf16[64,4,2048]{2,1,0:T(4,128)(2,1)}, u32[]{:S(2)}, u32[]{:S(2)}) async-start(bf16[64,4,2048]{2,1,0:T(4,128)(2,1)} %all_to_all.30), calls=%async_computation.1 | async-start | bytes 2097152 | tf_op jit(solution)/shard_map/all_to_all | solution.py:13
  154.4 1.4 all_to_all.37
  155.7 1.7 gather_fusion.3
  157.5 24.2 %all-to-all-done.1 = bf16[64,4,2048]{2,1,0:T(4,128)(2,1)} async-done(((bf16[64,4,2048]{2,1,0:T(4,128)(2,1)}), bf16[64,4,2048]{2,1,0:T(4,128)(2,1)}, u32[]{:S(2)}, u32[]{:S(2)}) %all-to-all-start.1) | async-done | bytes 1048608 | tf_op jit(solution)/shard_map/all_to_all | solution.py:13
  181.6 1.3 all_to_all.32
  183.0 0.9 gather_fusion.1
  183.9 2.6 %fusion.16 = (f32[128]{0:T(128)}, bf16[128,2048]{1,0:T(8,128)(2,1)}) fusion(bf16[128,2048]{1,0:T(8,128)(2,1)S(1)} %gather_fusion.1, bf16[128,2048]{1,0:T(8,128)(2,1)} %param.10, f32[128]{0:T(128)S(1)} %bitcast.53), kind=kLoop, calls=%fused_computation.30 | loop fusion | flops 1572736 | bytes 1573888 | tf_op jit(solution)/shard_map/reduce_sum | solution.py:70
  186.5 1.8 slice_bitcast_fusion
  (33 shorter events, 5.1 us)
Async XLA Ops:
  7.2 92.0 %copy-start = (bf16[1,384,2048]{2,1,0:T(8,128)(2,1)S(1)}, bf16[1,384,2048]{2,1,0:T(8,128)(2,1)}, u32[]{:S(2)}) copy-start(bf16[1,384,2048]{2,1,0:T(8,128)(2,1)} %param.13) | copy-start | bytes 4718596
  13.3 1.3 copy-start.1
  61.9 35.1 %all-to-all-start.2 = ((bf16[64,4,2048]{2,1,0:T(4,128)(2,1)}), bf16[64,4,2048]{2,1,0:T(4,128)(2,1)}, u32[]{:S(2)}, u32[]{:S(2)}) async-start(bf16[64,4,2048]{2,1,0:T(4,128)(2,1)} %get-tuple-element.14), calls=%async_computation.2 | async-start | bytes 2097152 | tf_op jit(solution)/shard_map/all_to_all | solution.py:13
  69.7 116.8 %reduce-scatter.2.cloned.1.call-start = ((), (), s32[]{:S(2)}) async-start(), calls=%async_computation.5 | async-start | bytes 5111808 | tf_op jit(solution)/shard_map/reduce_scatter | solution.py:81
  71.1 3.0 %copy-start.3 = (bf16[1,2048,384]{2,1,0:T(8,128)(2,1)S(1)}, bf16[1,2048,384]{2,1,0:T(8,128)(2,1)}, u32[]{:S(2)}) copy-start(bf16[1,2048,384]{2,1,0:T(8,128)(2,1)} %param.12) | copy-start | bytes 4718596
  101.4 1.2 copy-start.7
  102.0 1.2 copy-start.6
  106.3 1.4 copy-start.2
  107.7 1.8 copy-start.4
  111.5 35.1 %all-to-all-start.3 = ((bf16[64,4,2048]{2,1,0:T(4,128)(2,1)}), bf16[64,4,2048]{2,1,0:T(4,128)(2,1)S(1)}, u32[]{:S(2)}, u32[]{:S(2)}) async-start(bf16[64,4,2048]{2,1,0:T(4,128)(2,1)} %all_to_all.35), calls=%async_computation.3 | async-start | bytes 2097152 | tf_op jit(solution)/shard_map/all_to_all | solution.py:13
  146.6 7.7 %copy-start.5 = (bf16[64,4,2048]{2,1,0:T(4,128)(2,1)}, bf16[64,4,2048]{2,1,0:T(4,128)(2,1)S(1)}, u32[]{:S(2)}) copy-start(bf16[64,4,2048]{2,1,0:T(4,128)(2,1)S(1)} %all-to-all-done.3) | copy-start | bytes 3145732
  146.6 35.0 %all-to-all-start.1 = ((bf16[64,4,2048]{2,1,0:T(4,128)(2,1)}), bf16[64,4,2048]{2,1,0:T(4,128)(2,1)}, u32[]{:S(2)}, u32[]{:S(2)}) async-start(bf16[64,4,2048]{2,1,0:T(4,128)(2,1)} %all_to_all.30), calls=%async_computation.1 | async-start | bytes 2097152 | tf_op jit(solution)/shard_map/all_to_all | solution.py:13
  183.0 1.0 copy-start.8
Sparse Core Ops, SparseCore 0:
  106.4 71.3 reduce-scatter.1
where the time goes:
time: 197 us; the launch traced here: 195 us
  waiting for transfers between devices  69 us (35%)
  blocking collectives  41 us (21%)
  starting transfers between devices  23.3 us (12%)
  local copies, waits for them, and re-layouts  22.4 us (11%)
  between operations  14.3 us (7%)
  matrix products  12.7 us (6%)
  other arithmetic  12.4 us (6%)
    all_to_all x3, waiting for transfers between devices, move_rows(): lax.all_to_all(buffer, ('node', 'local'), split_axis=0, concat_axis=0, ti...  69 us
    all_to_all x1, blocking collectives, move_rows(): lax.all_to_all(buffer, ('node', 'local'), split_axis=0, concat_axis=0, ti...  41 us
    all_to_all x3, starting transfers between devices, move_rows(): lax.all_to_all(buffer, ('node', 'local'), split_axis=0, concat_axis=0, ti...  23.3 us
    all_to_all x6, local copies, waits for them, and re-layouts, move_rows(): lax.all_to_all(buffer, ('node', 'local'), split_axis=0, concat_axis=0, ti...  9.71 us
    dot_general x3, matrix products, contract_cols(): lax.dot_general(factor, operand, (((1,), (1,)), ((), ())), preferred_elem...  4.75 us
  transfers between devices with their start and end apart: 4, of which 3 were waited for; matrix products, arithmetic and copies ran while one was open for 7% of the time, Pallas kernels for 0%

commit v1 on v0

v1 whole, which is shorter than its diff:
```python
import functools

import jax
import jax.numpy as jnp
from jax import lax
from jax.experimental import pallas as pl
from jax.experimental.pallas import tpu as pltpu
from jax.sharding import PartitionSpec as P

BF16 = jnp.bfloat16
F32 = jnp.float32
VMEM = pl.BlockSpec(memory_space=pltpu.VMEM)


def dot(a, b, da, db):
    return lax.dot_general(a, b, (((da,), (db,)), ((), ())), preferred_element_type=F32)


def iota(shape, dim):
    return lax.broadcasted_iota(jnp.int32, shape, dim)


def slots_of(ids, experts, capacity):
    tok = ids.shape[1]
    named = iota((experts, tok), 0) == ids
    before = (iota((tok, tok), 0) < iota((tok, tok), 1)).astype(BF16)
    rank = dot(named.astype(BF16), before, 1, 0)
    place = jnp.sum(jnp.where(named, rank, 0.0), axis=0, keepdims=True).astype(jnp.int32)
    return ids * (2 * capacity) + place


def column_of(row):
    tok = row.shape[1]
    eye = iota((tok, tok), 0) == iota((tok, tok), 1)
    return jnp.sum(jnp.where(eye, row, 0.0), axis=1, keepdims=True)


def hot(target, rows):
    return (iota((rows, target.shape[1]), 0) == target).astype(F32).astype(BF16)


def dispatch_kernel(experts, capacity, ids_ref, gates_ref, tokens_ref, grad_ref, out_ref):
    target = slots_of(ids_ref[...], experts, capacity)
    gates = column_of(gates_ref[...])
    scaled = (gates * grad_ref[...].astype(F32)).astype(BF16)
    rows = 2 * capacity * experts
    out = dot(hot(target, rows), tokens_ref[...], 1, 0)
    out += dot(hot(target + capacity, rows), scaled, 1, 0)
    out_ref[...] = out.astype(BF16)


def pick(rows, capacity, kind):
    at, of = iota((rows, 2 * rows), 0), iota((rows, 2 * rows), 1)
    return (of == at + (at // capacity + kind) * capacity).astype(F32).astype(BF16)


def terms_kernel(
    capacity, parts, in_ref, gate_ref, up_ref, down_ref, terms_ref, hidden_ref, dgate_ref, dup_ref
):
    rows = in_ref.shape[0] // 2
    both = in_ref[...]
    incoming = dot(pick(rows, capacity, 0), both, 1, 0).astype(BF16)
    expert_grad = dot(pick(rows, capacity, 1), both, 1, 0).astype(BF16)
    pre_gate = dot(incoming, gate_ref[0], 1, 0)
    pre_up = dot(incoming, up_ref[0], 1, 0)
    sigma = jax.nn.sigmoid(pre_gate)
    activated = pre_gate * sigma
    slope = sigma * (1.0 + pre_gate * (1.0 - sigma))
    hidden = (activated * pre_up).astype(BF16)
    grad_hidden = dot(expert_grad, down_ref[0], 1, 1)
    dgate = (grad_hidden * pre_up * slope).astype(BF16)
    dup = (grad_hidden * activated).astype(BF16)
    hidden_ref[...] = hidden
    dgate_ref[...] = dgate
    dup_ref[...] = dup
    for k, (factor, operand) in enumerate(
        ((dgate, incoming), (dup, incoming), (hidden, expert_grad))
    ):
        term = dot(factor, operand, 0, 0).astype(BF16)
        terms_ref[:, k] = term.reshape(parts, term.shape[0] // parts, term.shape[1])


def returns_kernel(capacity, hidden_ref, dgate_ref, dup_ref, gate_ref, up_ref, down_ref, out_ref):
    rows = hidden_ref.shape[0]
    back = dot(hidden_ref[...], down_ref[0], 1, 0).astype(BF16)
    grad = (
        dot(dgate_ref[...], gate_ref[0], 1, 1) + dot(dup_ref[...], up_ref[0], 1, 1)
    ).astype(BF16)
    out = dot(pick(rows, capacity, 0), back, 0, 0) + dot(pick(rows, capacity, 1), grad, 0, 0)
    out_ref[...] = out.astype(BF16)


def combine_kernel(
    experts, capacity, ids_ref, gates_ref, grad_ref, back_ref, out_ref, dtok_ref, dgates_ref
):
    target = slots_of(ids_ref[...], experts, capacity)
    gates = column_of(gates_ref[...])
    rows = 2 * capacity * experts
    back = back_ref[...]
    slot_out = dot(hot(target, rows), back, 0, 0)
    dtok_ref[...] = dot(hot(target + capacity, rows), back, 0, 0).astype(BF16)
    out_ref[...] = (gates * slot_out).astype(BF16)
    value = jnp.sum(grad_ref[...].astype(F32) * slot_out, axis=1, keepdims=True)
    tok = value.shape[0]
    eye = iota((tok, tok), 0) == iota((tok, tok), 1)
    dgates_ref[...] = jnp.sum(jnp.where(eye, value, 0.0), axis=0, keepdims=True)


def call(kernel, out_shape, n_in, flops, traffic, name):
    many = isinstance(out_shape, (tuple, list))
    return pl.pallas_call(
        kernel,
        out_shape=out_shape,
        in_specs=[VMEM] * n_in,
        out_specs=[VMEM] * len(out_shape) if many else VMEM,
        compiler_params=pltpu.CompilerParams(vmem_limit_bytes=32 * 2**20),
        cost_estimate=pl.CostEstimate(flops=flops, bytes_accessed=traffic, transcendentals=0),
        name=name,
    )


def move_rows(buffer):
    return lax.all_to_all(buffer, ("node", "local"), split_axis=0, concat_axis=0, tiled=True)


def on_device(tokens, expert_ids, gates, out_grad, w_gate, w_up, w_down):
    experts = lax.axis_size("node") * lax.axis_size("local")
    parts = lax.axis_size("dp")
    tok, width = tokens.shape
    units = w_gate.shape[2]
    capacity = max(2, 2 * tok // experts)
    rows = experts * capacity
    sds = jax.ShapeDtypeStruct
    ids = expert_ids.reshape(1, tok)
    gate_row = gates.reshape(1, tok)
    outgoing = call(
        functools.partial(dispatch_kernel, experts, capacity),
        sds((2 * rows, width), BF16), 4, 8 * rows * tok * width, 8 * tok * width, "dispatch",
    )(ids, gate_row, tokens, out_grad)
    incoming = move_rows(outgoing.reshape(experts, 2 * capacity, width)).reshape(2 * rows, width)
    small = sds((rows, units), BF16)
    terms, hidden, dgate, dup = call(
        functools.partial(terms_kernel, capacity, parts),
        (sds((parts, 3, units // parts, width), BF16), small, small, small),
        4, 18 * rows * width * units, 10 * width * units + 4 * rows * width, "terms",
    )(incoming, w_gate, w_up, w_down)
    shares = lax.psum_scatter(
        terms.reshape(3 * units, width), "dp", scatter_dimension=0, tiled=True
    )
    back = call(
        functools.partial(returns_kernel, capacity),
        sds((2 * rows, width), BF16), 6, 10 * rows * width * units,
        6 * width * units + 4 * rows * width, "returns",
    )(hidden, dgate, dup, w_gate, w_up, w_down)
    back = move_rows(back.reshape(experts, 2 * capacity, width)).reshape(2 * rows, width)
    layer_out, grad_in, grad_gates = call(
        functools.partial(combine_kernel, experts, capacity),
        (sds((tok, width), BF16), sds((tok, width), BF16), sds((1, tok), F32)),
        4, 8 * rows * tok * width, 10 * tok * width, "combine",
    )(ids, gate_row, out_grad, back)
    part = units // parts
    return (
        layer_out,
        grad_in,
        grad_gates.reshape(tok, 1),
        shares[None, :part],
        shares[None, part : 2 * part],
        shares[None, 2 * part :],
    )


def solution(mesh):
    by_token = P(("dp", "node", "local"), None)
    by_expert = P(("node", "local"), None, None)
    by_share = P(("node", "local"), "dp", None)
    return jax.shard_map(
        on_device,
        mesh=mesh,
        in_specs=(by_token,) * 4 + (by_expert,) * 3,
        out_specs=(by_token,) * 3 + (by_share,) * 3,
        check_vma=False,
    )
```

time: 197 us -> 164 us (0.83)
  blocking collectives: 41 us -> 120 us
  waiting for transfers between devices: 69 us -> 8.79 us
  starting transfers between devices: 23.3 us -> 0.04 us
  matrix products: 12.7 us -> 0 us
  other arithmetic: 12.4 us -> 0 us
  local copies, waits for them, and re-layouts: 22.4 us -> 10.3 us
  Pallas kernels: 0 us -> 10.4 us
    all_to_all x1 -> x2, blocking collectives: 41 us -> 120 us  [move_rows(): lax.all_to_all(buffer, ('node', 'local'), split_axis=0, concat_axis=0, ti...]
    all_to_all x3 -> x0, waiting for transfers between devices: 69 us -> none  [move_rows(): lax.all_to_all(buffer, ('node', 'local'), split_axis=0, concat_axis=0, ti...]
    all_to_all x3 -> x0, starting transfers between devices: 23.3 us -> none  [move_rows(): lax.all_to_all(buffer, ('node', 'local'), split_axis=0, concat_axis=0, ti...]
    dot_general x9 -> x0, matrix products: 12.7 us -> none  [the longest x3 4.75 us: contract_cols(): lax.dot_general(factor, operand, (((1,), (1,)), ((), ())), preferred_elem...]
    pallas_call x0 -> x4, Pallas kernels: none -> 10.4 us  [the longest x1 4.37 us: on_device(): call(functools.partial(terms_kernel, capacity, parts), (sds((parts, 3, un...]
    all_to_all x6 -> x0, local copies, waits for them, and re-layouts: 9.71 us -> none  [move_rows(): lax.all_to_all(buffer, ('node', 'local'), split_axis=0, concat_axis=0, ti...]
    reduce_scatter x1, waiting for transfers between devices: 0.01 us -> 8.77 us  [on_device(): lax.psum_scatter(terms.reshape(3 * units, width), 'dp', scatter_dimension...]
    gather x6 -> x0, local copies, waits for them, and re-layouts: 7.84 us -> none  [the longest x2 2.6 us: on_device(): scaled[clipped]]
  transfers between devices with their start and end apart: 4 -> 1, of which waited for: 3 -> 1; matrix products, arithmetic and copies ran while one was open for 7% -> 0% of each run, Pallas kernels for 0% -> 3%
where the time goes in v1:
time: 164 us; the launch traced here: 163 us
  blocking collectives  120 us (73%)
  between operations  14.1 us (9%)
  Pallas kernels  10.4 us (6%)
  local copies, waits for them, and re-layouts  10.3 us (6%)
  waiting for transfers between devices  8.79 us (5%)
    all_to_all x2, blocking collectives, move_rows(): lax.all_to_all(buffer, ('node', 'local'), split_axis=0, concat_axis=0, ti...  120 us
    reduce_scatter x1, waiting for transfers between devices, on_device(): lax.psum_scatter(terms.reshape(3 * units, width), 'dp', scatter_dimension...  8.77 us
    unnamed x28, local copies, waits for them, and re-layouts  8.55 us
    pallas_call x1, Pallas kernels, on_device(): call(functools.partial(terms_kernel, capacity, parts), (sds((parts, 3, un...  4.37 us
  transfers between devices with their start and end apart: 1, of which 1 were waited for; matrix products, arithmetic and copies ran while one was open for 0% of the time, Pallas kernels for 3%

profile of v1, /device:TPU:6, one launch (start us, length us, event | category | flops | bytes accessed | tf_op | source)
XLA Modules:
  0.0 163.2 jit_solution(4139577868619977927)
XLA Ops:
  7.2 0.0 reduce-scatter.2.cloned.1.call-start
  7.2 0.0 copy-start.1
  7.2 1.0 copy-done.1
  8.3 1.0 copy-done.3
  9.3 0.7 copy-done.4
  10.0 0.7 copy-done.6
  10.6 1.4 dispatch.1
  12.0 0.0 copy-start.8
  12.0 0.0 copy-start.9
  12.0 62.0 %all_to_all.10 = bf16[64,8,2048]{2,1,0:T(8,128)(2,1)S(1)} all-to-all(bf16[64,8,2048]{2,1,0:T(8,128)(2,1)S(1)} %bitcast.15), channel_id=1, replica_groups=mesh['dp'=12,'node'=8,'local'=8] {'node','local'}, dimensions={0} | all-to-all | bytes 4194304 | tf_op jit(solution)/shard_map/all_to_all | solution.py:123
  74.1 0.0 copy-done.10
  74.1 0.0 copy-done.8
  74.1 0.0 copy-done.9
  74.1 4.4 %terms.1 = (bf16[12,3,32,2048]{3,2,1,0:T(8,128)(2,1)S(1)}, bf16[256,384]{1,0:T(8,128)(2,1)S(1)}, bf16[256,384]{1,0:T(8,128)(2,1)S(1)}, bf16[256,384]{1,0:T(8,128)(2,1)S(1)}) custom-call(bf16[512,2048]{1,0:T(8,128)(2,1)S(1)} %bitcast.17, bf16[1,2048,384]{2,1,0:T(8,128)(2,1)S(1)} %copy-done.8, bf16[1,2048,384]{2,1,0:T(8,128)(2,1)S(1)} %copy-done.9, ...), custom_call_target="tpu_custom_call" | custom-call | flops 3623878656 | bytes 9961472 | tf_op jit(solution)/shard_map/terms/pallas_call | solution.py:142
  78.5 0.0 copy-start
  78.5 2.1 %copy-done = bf16[12,3,32,2048]{3,2,1,0:T(8,128)(2,1)} copy-done((bf16[12,3,32,2048]{3,2,1,0:T(8,128)(2,1)}, bf16[12,3,32,2048]{3,2,1,0:T(8,128)(2,1)S(1)}, u32[]{:S(2)}) %copy-start) | copy-done | bytes 4718616
  80.6 0.7 copy-done.12
  81.3 0.0 reduce-scatter.2.cloned.1.call-update
  81.3 0.0 copy-start.11
  81.3 1.4 copy-done.11
  82.7 0.9 copy-done.13
  83.6 2.9 %returns.1 = bf16[512,2048]{1,0:T(8,128)(2,1)S(1)} custom-call(bf16[256,384]{1,0:T(8,128)(2,1)S(1)} %get-tuple-element.13.hidden_ref, bf16[256,384]{1,0:T(8,128)(2,1)S(1)} %get-tuple-element.14.dgate_ref, bf16[256,384]{1,0:T(8,128)(2,1)S(1)} %copy-done.13, bf16[1,2048,384]{2,1,0:T(8,128)(2,1)S(1)} %copy-done.8, bf16[1,2048,384]{2,1,0:T(8,128)(2,1)S(1)} %copy-done.9, ...), custom_call_target="tpu_custom_call" | custom-call | flops 2013265920 | bytes 6815744 | tf_op jit(solution)/shard_map/returns/pallas_call | solution.py:150
  86.5 0.0 copy-start.2
  86.6 0.0 copy-start.5
  86.6 0.0 copy-start.7
  86.6 57.5 %all_to_all.11 = bf16[64,8,2048]{2,1,0:T(8,128)(2,1)S(1)} all-to-all(bf16[64,8,2048]{2,1,0:T(8,128)(2,1)S(1)} %bitcast.18), channel_id=1, replica_groups=mesh['dp'=12,'node'=8,'local'=8] {'node','local'}, dimensions={0} | all-to-all | bytes 4194304 | tf_op jit(solution)/shard_map/all_to_all | solution.py:123
  144.1 0.0 copy-done.2
  144.1 0.0 copy-done.5
  144.1 0.0 copy-done.7
  144.1 1.7 %combine.1 = (bf16[128,2048]{1,0:T(8,128)(2,1)}, bf16[128,2048]{1,0:T(8,128)(2,1)}, f32[1,128]{1,0:T(1,128)}) custom-call(s32[1,128]{1,0:T(1,128)S(1)} %bitcast.20, f32[1,128]{1,0:T(1,128)S(1)} %bitcast.22, bf16[128,2048]{1,0:T(8,128)(2,1)S(1)} %copy-done.2, bf16[512,2048]{1,0:T(8,128)(2,1)S(1)} %bitcast.14), custom_call_target="tpu_custom_call" | custom-call | flops 536870912 | bytes 2621440 | tf_op jit(solution)/shard_map/combine/pallas_call | solution.py:156
  145.8 8.8 %reduce-scatter.2.cloned.1.call-done = bf16[96,2048]{1,0:T(8,128)(2,1)} async-done(((bf16[1152,2048]{1,0:T(8,128)(2,1)}), bf16[96,2048]{1,0:T(8,128)(2,1)}) %reduce-scatter.2.cloned.1.call-update) | async-done | bytes 393232 | tf_op jit(solution)/shard_map/reduce_scatter | solution.py:147
  154.6 1.8 %slice_bitcast_fusion = (bf16[1,32,2048]{2,1,0:T(8,128)(2,1)}, bf16[1,32,2048]{2,1,0:T(8,128)(2,1)}, bf16[1,32,2048]{2,1,0:T(8,128)(2,1)}) fusion(bf16[96,2048]{1,0:T(8,128)(2,1)} %reduce-scatter.2.cloned.1.call-done), kind=kLoop, calls=%fused_computation | loop fusion | bytes 786432 | tf_op jit(solution)/shard_map/broadcast_in_dim | solution.py:168
  (6 shorter events, 0.0 us)
Async XLA Ops:
  7.2 147.4 %reduce-scatter.2.cloned.1.call-start = ((), (), s32[]{:S(2)}) async-start(), calls=%async_computation.3 | async-start | bytes 5111808 | tf_op jit(solution)/shard_map/reduce_scatter | solution.py:147
  7.2 1.0 copy-start.1
  8.3 1.0 copy-start.3
  9.3 0.7 copy-start.4
  10.0 0.7 copy-start.6
  10.6 63.5 %copy-start.10 = (bf16[1,384,2048]{2,1,0:T(8,128)(2,1)S(1)}, bf16[1,384,2048]{2,1,0:T(8,128)(2,1)}, u32[]{:S(2)}) copy-start(bf16[1,384,2048]{2,1,0:T(8,128)(2,1)} %down_ref.3) | copy-start | bytes 4718596
  12.0 62.1 %copy-start.8 = (bf16[1,2048,384]{2,1,0:T(8,128)(2,1)S(1)}, bf16[1,2048,384]{2,1,0:T(8,128)(2,1)}, u32[]{:S(2)}) copy-start(bf16[1,2048,384]{2,1,0:T(8,128)(2,1)} %gate_ref.3) | copy-start | bytes 4718596
  12.0 62.1 %copy-start.9 = (bf16[1,2048,384]{2,1,0:T(8,128)(2,1)S(1)}, bf16[1,2048,384]{2,1,0:T(8,128)(2,1)}, u32[]{:S(2)}) copy-start(bf16[1,2048,384]{2,1,0:T(8,128)(2,1)} %up_ref.3) | copy-start | bytes 4718596
  78.5 2.1 %copy-start = (bf16[12,3,32,2048]{3,2,1,0:T(8,128)(2,1)}, bf16[12,3,32,2048]{3,2,1,0:T(8,128)(2,1)S(1)}, u32[]{:S(2)}) copy-start(bf16[12,3,32,2048]{3,2,1,0:T(8,128)(2,1)S(1)} %get-tuple-element.19) | copy-start | bytes 14155780
  80.6 0.7 copy-start.12
  81.3 1.4 copy-start.11
  82.7 0.9 copy-start.13
  86.5 57.5 %copy-start.2 = (bf16[128,2048]{1,0:T(8,128)(2,1)S(1)}, bf16[128,2048]{1,0:T(8,128)(2,1)}, u32[]{:S(2)}) copy-start(bf16[128,2048]{1,0:T(8,128)(2,1)} %grad_ref.3) | copy-start | bytes 1572868
  86.6 57.5 %copy-start.5 = (s32[128,1]{0,1:T(1,128)S(1)}, s32[128,1]{0,1:T(1,128)}, u32[]{:S(2)}) copy-start(s32[128,1]{0,1:T(1,128)} %param.8) | copy-start | bytes 1540
  86.6 57.5 %copy-start.7 = (f32[128,1]{0,1:T(1,128)S(1)}, f32[128,1]{0,1:T(1,128)}, u32[]{:S(2)}) copy-start(f32[128,1]{0,1:T(1,128)} %param.9) | copy-start | bytes 1540
Sparse Core Ops, SparseCore 0:
  81.4 73.1 reduce-scatter.1

commit v2 on v1

--- a/solution.py
+++ b/solution.py
@@ -10,6 +10,7 @@
 BF16 = jnp.bfloat16
 F32 = jnp.float32
 VMEM = pl.BlockSpec(memory_space=pltpu.VMEM)
+HBM = pl.BlockSpec(memory_space=pltpu.HBM)
 
 
 def dot(a, b, da, db):
@@ -39,13 +40,29 @@
     return (iota((rows, target.shape[1]), 0) == target).astype(F32).astype(BF16)
 
 
-def dispatch_kernel(experts, capacity, ids_ref, gates_ref, tokens_ref, grad_ref, out_ref):
+def dispatch_kernel(
+    experts, capacity, ids_hbm, gates_hbm, tokens_hbm, grad_hbm, out_ref,
+    ids_ref, gates_ref, tokens_ref, grad_ref, sems,
+):
+    loads = [
+        pltpu.make_async_copy(src, dst, sems.at[i])
+        for i, (src, dst) in enumerate((
+            (ids_hbm, ids_ref), (gates_hbm, gates_ref), (tokens_hbm, tokens_ref), (grad_hbm, grad_ref)
+        ))
+    ]
+    for load in loads:
+        load.start()
+    loads[0].wait()
     target = slots_of(ids_ref[...], experts, capacity)
+    rows = 2 * capacity * experts
+    to_token, to_grad = hot(target, rows), hot(target + capacity, rows)
+    loads[1].wait()
     gates = column_of(gates_ref[...])
+    loads[2].wait()
+    out = dot(to_token, tokens_ref[...], 1, 0)
+    loads[3].wait()
     scaled = (gates * grad_ref[...].astype(F32)).astype(BF16)
-    rows = 2 * capacity * experts
-    out = dot(hot(target, rows), tokens_ref[...], 1, 0)
-    out += dot(hot(target + capacity, rows), scaled, 1, 0)
+    out += dot(to_grad, scaled, 1, 0)
     out_ref[...] = out.astype(BF16)
 
 
@@ -55,14 +72,15 @@
 
 
 def terms_kernel(
-    capacity, parts, in_ref, gate_ref, up_ref, down_ref, terms_ref, hidden_ref, dgate_ref, dup_ref
+    capacity, parts, in_ref, gate_ref, up_ref, down_ref, terms_hbm, factors_hbm,
+    terms_ref, factors_ref, sems,
 ):
     rows = in_ref.shape[0] // 2
     both = in_ref[...]
     incoming = dot(pick(rows, capacity, 0), both, 1, 0).astype(BF16)
-    expert_grad = dot(pick(rows, capacity, 1), both, 1, 0).astype(BF16)
     pre_gate = dot(incoming, gate_ref[0], 1, 0)
     pre_up = dot(incoming, up_ref[0], 1, 0)
+    expert_grad = dot(pick(rows, capacity, 1), both, 1, 0).astype(BF16)
     sigma = jax.nn.sigmoid(pre_gate)
     activated = pre_gate * sigma
     slope = sigma * (1.0 + pre_gate * (1.0 - sigma))
@@ -70,21 +88,38 @@
     grad_hidden = dot(expert_grad, down_ref[0], 1, 1)
     dgate = (grad_hidden * pre_up * slope).astype(BF16)
     dup = (grad_hidden * activated).astype(BF16)
-    hidden_ref[...] = hidden
-    dgate_ref[...] = dgate
-    dup_ref[...] = dup
+    units = hidden.shape[1]
+    for k, factor in enumerate((dgate, dup, hidden)):
+        factors_ref[:, k * units : (k + 1) * units] = factor
+    stores = [pltpu.make_async_copy(factors_ref, factors_hbm, sems.at[3])]
+    stores[0].start()
     for k, (factor, operand) in enumerate(
         ((dgate, incoming), (dup, incoming), (hidden, expert_grad))
     ):
         term = dot(factor, operand, 0, 0).astype(BF16)
         terms_ref[:, k] = term.reshape(parts, term.shape[0] // parts, term.shape[1])
-
-
-def returns_kernel(capacity, hidden_ref, dgate_ref, dup_ref, gate_ref, up_ref, down_ref, out_ref):
-    rows = hidden_ref.shape[0]
-    back = dot(hidden_ref[...], down_ref[0], 1, 0).astype(BF16)
+        stores.append(pltpu.make_async_copy(terms_ref.at[:, k], terms_hbm.at[:, k], sems.at[k]))
+        stores[-1].start()
+    for store in stores:
+        store.wait()
+
+
+def returns_kernel(
+    capacity, factors_hbm, gate_ref, up_ref, down_hbm, out_ref, factors_ref, down_ref, sems
+):
+    loads = (
+        pltpu.make_async_copy(factors_hbm, factors_ref, sems.at[0]),
+        pltpu.make_async_copy(down_hbm, down_ref, sems.at[1]),
+    )
+    for load in loads:
+        load.start()
+    for load in loads:
+        load.wait()
+    rows, units = factors_ref.shape[0], gate_ref.shape[2]
+    dgate, dup, hidden = (factors_ref[:, k * units : (k + 1) * units] for k in range(3))
+    back = dot(hidden, down_ref[0], 1, 0).astype(BF16)
     grad = (
-        dot(dgate_ref[...], gate_ref[0], 1, 1) + dot(dup_ref[...], up_ref[0], 1, 1)
+        dot(dgate, gate_ref[0], 1, 1) + dot(dup, up_ref[0], 1, 1)
     ).astype(BF16)
     out = dot(pick(rows, capacity, 0), back, 0, 0) + dot(pick(rows, capacity, 1), grad, 0, 0)
     out_ref[...] = out.astype(BF16)
@@ -106,17 +141,34 @@
     dgates_ref[...] = jnp.sum(jnp.where(eye, value, 0.0), axis=0, keepdims=True)
 
 
-def call(kernel, out_shape, n_in, flops, traffic, name):
-    many = isinstance(out_shape, (tuple, list))
+def split_kernel(in_hbm, *refs):
+    outs, sems = refs[:3], refs[3]
+    part = in_hbm.shape[0] // 3
+    copies = [
+        pltpu.make_async_copy(in_hbm.at[pl.ds(k * part, part)], out.at[0], sems.at[k])
+        for k, out in enumerate(outs)
+    ]
+    for copy in copies:
+        copy.start()
+    for copy in copies:
+        copy.wait()
+
+
+def call(kernel, out_shape, in_specs, out_specs, scratch, vmem_mib, flops, traffic, name):
     return pl.pallas_call(
         kernel,
         out_shape=out_shape,
-        in_specs=[VMEM] * n_in,
-        out_specs=[VMEM] * len(out_shape) if many else VMEM,
-        compiler_params=pltpu.CompilerParams(vmem_limit_bytes=32 * 2**20),
+        in_specs=in_specs,
+        out_specs=out_specs,
+        scratch_shapes=scratch,
+        compiler_params=pltpu.CompilerParams(vmem_limit_bytes=vmem_mib * 2**20),
         cost_estimate=pl.CostEstimate(flops=flops, bytes_accessed=traffic, transcendentals=0),
         name=name,
     )
+
+
+def in_hbm(*arrays):
+    return [pltpu.with_memory_space_constraint(a, pltpu.HBM) for a in arrays]
 
 
 def move_rows(buffer):
@@ -133,40 +185,42 @@
     sds = jax.ShapeDtypeStruct
     ids = expert_ids.reshape(1, tok)
     gate_row = gates.reshape(1, tok)
+    dma = pltpu.SemaphoreType.DMA
     outgoing = call(
         functools.partial(dispatch_kernel, experts, capacity),
-        sds((2 * rows, width), BF16), 4, 8 * rows * tok * width, 8 * tok * width, "dispatch",
-    )(ids, gate_row, tokens, out_grad)
+        sds((2 * rows, width), BF16), [HBM] * 4, VMEM,
+        [pltpu.VMEM((1, tok), jnp.int32), pltpu.VMEM((1, tok), F32)]
+        + [pltpu.VMEM((tok, width), BF16)] * 2 + [dma((4,))],
+        12, 8 * rows * tok * width, 8 * tok * width, "dispatch",
+    )(*in_hbm(ids, gate_row, tokens, out_grad))
     incoming = move_rows(outgoing.reshape(experts, 2 * capacity, width)).reshape(2 * rows, width)
-    small = sds((rows, units), BF16)
-    terms, hidden, dgate, dup = call(
+    blocks = (parts, 3, units // parts, width)
+    terms, factors = call(
         functools.partial(terms_kernel, capacity, parts),
-        (sds((parts, 3, units // parts, width), BF16), small, small, small),
-        4, 18 * rows * width * units, 10 * width * units + 4 * rows * width, "terms",
+        (pltpu.HBM(blocks, BF16), pltpu.HBM((rows, 3 * units), BF16)), [VMEM] * 4, [HBM] * 2,
+        [pltpu.VMEM(blocks, BF16), pltpu.VMEM((rows, 3 * units), BF16), dma((4,))],
+        20, 18 * rows * width * units, 10 * width * units + 4 * rows * width, "terms",
     )(incoming, w_gate, w_up, w_down)
     shares = lax.psum_scatter(
         terms.reshape(3 * units, width), "dp", scatter_dimension=0, tiled=True
     )
     back = call(
         functools.partial(returns_kernel, capacity),
-        sds((2 * rows, width), BF16), 6, 10 * rows * width * units,
-        6 * width * units + 4 * rows * width, "returns",
-    )(hidden, dgate, dup, w_gate, w_up, w_down)
+        sds((2 * rows, width), BF16), [HBM, VMEM, VMEM, HBM], VMEM,
+        [pltpu.VMEM((rows, 3 * units), BF16), pltpu.VMEM((1, units, width), BF16), dma((2,))], 16,
+        10 * rows * width * units, 6 * width * units + 4 * rows * width, "returns",
+    )(*in_hbm(factors), w_gate, w_up, *in_hbm(w_down))
     back = move_rows(back.reshape(experts, 2 * capacity, width)).reshape(2 * rows, width)
     layer_out, grad_in, grad_gates = call(
         functools.partial(combine_kernel, experts, capacity),
         (sds((tok, width), BF16), sds((tok, width), BF16), sds((1, tok), F32)),
-        4, 8 * rows * tok * width, 10 * tok * width, "combine",
+        [VMEM] * 4, [VMEM] * 3, [], 12, 8 * rows * tok * width, 10 * tok * width, "combine",
     )(ids, gate_row, out_grad, back)
-    part = units // parts
-    return (
-        layer_out,
-        grad_in,
-        grad_gates.reshape(tok, 1),
-        shares[None, :part],
-        shares[None, part : 2 * part],
-        shares[None, 2 * part :],
-    )
+    share = pltpu.HBM((1, units // parts, width), BF16)
+    grads = call(
+        split_kernel, (share,) * 3, [HBM], [HBM] * 3, [dma((3,))], 4, 0, 2 * 3 * units // parts * width, "split"
+    )(*in_hbm(shares))
+    return (layer_out, grad_in, grad_gates.reshape(tok, 1), *grads)
 
 
 def solution(mesh):

time: 164 us -> 171 us (1.043)
  Pallas kernels: 10.4 us -> 27.7 us
  local copies, waits for them, and re-layouts: 10.3 us -> 0.04 us
    pallas_call x1 -> x2, Pallas kernels: 4.37 us -> 18.7 us  [the longest x1 13 us: on_device(): call(split_kernel, (share,) * 3, [HBM], [HBM] * 3, [dma((3,))], 4, 0, 2 *...]
    unnamed x28 -> x12, local copies, waits for them, and re-layouts: 8.55 us -> 0.04 us
    broadcast_in_dim x1 -> x0, local copies, waits for them, and re-layouts: 1.78 us -> none  [on_device(): shares[None, 2 * part:]]
  transfers between devices with their start and end apart: 1 -> 1, of which waited for: 1 -> 1; matrix products, arithmetic and copies ran while one was open for 0% -> 0% of each run, Pallas kernels for 3% -> 4%
where the time goes in v2:
time: 171 us
  blocking collectives  120 us (70%)
  Pallas kernels  27.7 us (16%)
  between operations  14.1 us (8%)
  waiting for transfers between devices  9.55 us (6%)
    all_to_all x2, blocking collectives, move_rows(): lax.all_to_all(buffer, ('node', 'local'), split_axis=0, concat_axis=0, ti...  120 us
    pallas_call x1, Pallas kernels, on_device(): call(split_kernel, (share,) * 3, [HBM], [HBM] * 3, [dma((3,))], 4, 0, 2 *...  13 us
    reduce_scatter x1, waiting for transfers between devices, on_device(): lax.psum_scatter(terms.reshape(3 * units, width), 'dp', scatter_dimension...  9.53 us
    pallas_call x1, Pallas kernels, on_device(): call(functools.partial(terms_kernel, capacity, parts), (pltpu.HBM(blocks,...  5.71 us
    pallas_call x1, Pallas kernels, on_device(): call(functools.partial(returns_kernel, capacity), sds((2 * rows, width),...  4.51 us
  transfers between devices with their start and end apart: 1, of which 1 were waited for; matrix products, arithmetic and copies ran while one was open for 0% of the time, Pallas kernels for 4%

profile of v2, /device:TPU:6, one launch (start us, length us, event | category | flops | bytes accessed | tf_op | source)
XLA Modules:
  0.0 171.0 jit_solution(12346448909461766000)
XLA Ops:
  7.2 0.0 reduce-scatter.2.cloned.1.call-start
  7.2 0.0 copy-start.5
  7.2 2.6 %dispatch.1 = bf16[512,2048]{1,0:T(8,128)(2,1)S(1)} custom-call(s32[1,128]{1,0:T(1,128)} %bitcast.12, f32[1,128]{1,0:T(1,128)} %bitcast.14, bf16[128,2048]{1,0:T(8,128)(2,1)} %tokens_hbm.1, bf16[128,2048]{1,0:T(8,128)(2,1)} %grad_ref.1), custom_call_target="tpu_custom_call" | custom-call | flops 536870912 | bytes 2097152 | tf_op jit(solution)/shard_map/dispatch/pallas_call | solution.py:189
  9.9 0.0 copy-start.3
  9.9 0.0 copy-start.4
  9.9 62.0 %all_to_all.10 = bf16[64,8,2048]{2,1,0:T(8,128)(2,1)S(1)} all-to-all(bf16[64,8,2048]{2,1,0:T(8,128)(2,1)S(1)} %bitcast.9), channel_id=1, replica_groups=mesh['dp'=12,'node'=8,'local'=8] {'node','local'}, dimensions={0} | all-to-all | bytes 4194304 | tf_op jit(solution)/shard_map/all_to_all | solution.py:175
  71.9 0.0 copy-done.5
  71.9 0.0 copy-done.3
  71.9 0.0 copy-done.4
  71.9 5.7 %terms.1 = (bf16[12,3,32,2048]{3,2,1,0:T(8,128)(2,1)}, bf16[256,1152]{1,0:T(8,128)(2,1)}) custom-call(bf16[512,2048]{1,0:T(8,128)(2,1)S(1)} %bitcast.10, bf16[1,2048,384]{2,1,0:T(8,128)(2,1)S(1)} %copy-done.3, bf16[1,2048,384]{2,1,0:T(8,128)(2,1)S(1)} %copy-done.4, bf16[1,384,2048]{2,1,0:T(8,128)(2,1)S(1)} %copy-done.5), custom_call_target="tpu_custom_call" | custom-call | flops 3623878656 | bytes 9961472 | tf_op jit(solution)/shard_map/terms/pallas_call | solution.py:198
  77.7 0.0 reduce-scatter.2.cloned.1.call-update
  77.7 4.5 %returns.1 = bf16[512,2048]{1,0:T(8,128)(2,1)S(1)} custom-call(bf16[256,1152]{1,0:T(8,128)(2,1)} %get-tuple-element.14.factors_hbm, bf16[1,2048,384]{2,1,0:T(8,128)(2,1)S(1)} %copy-done.3, bf16[1,2048,384]{2,1,0:T(8,128)(2,1)S(1)} %copy-done.4, bf16[1,384,2048]{2,1,0:T(8,128)(2,1)} %down_hbm.1), custom_call_target="tpu_custom_call" | custom-call | flops 2013265920 | bytes 6815744 | tf_op jit(solution)/shard_map/returns/pallas_call | solution.py:207
  82.2 0.0 copy-start
  82.2 0.0 copy-start.1
  82.2 0.0 copy-start.2
  82.2 57.5 %all_to_all.11 = bf16[64,8,2048]{2,1,0:T(8,128)(2,1)S(1)} all-to-all(bf16[64,8,2048]{2,1,0:T(8,128)(2,1)S(1)} %bitcast.11), channel_id=1, replica_groups=mesh['dp'=12,'node'=8,'local'=8] {'node','local'}, dimensions={0} | all-to-all | bytes 4194304 | tf_op jit(solution)/shard_map/all_to_all | solution.py:175
  139.7 0.0 copy-done
  139.7 0.0 copy-done.1
  139.7 0.0 copy-done.2
  139.8 1.8 %combine.1 = (bf16[128,2048]{1,0:T(8,128)(2,1)}, bf16[128,2048]{1,0:T(8,128)(2,1)}, f32[1,128]{1,0:T(1,128)}) custom-call(s32[1,128]{1,0:T(1,128)S(1)} %bitcast.13, f32[1,128]{1,0:T(1,128)S(1)} %bitcast.15, bf16[128,2048]{1,0:T(8,128)(2,1)S(1)} %copy-done, bf16[512,2048]{1,0:T(8,128)(2,1)S(1)} %bitcast.8), custom_call_target="tpu_custom_call" | custom-call | flops 536870912 | bytes 2621440 | tf_op jit(solution)/shard_map/combine/pallas_call | solution.py:214
  141.5 9.5 %reduce-scatter.2.cloned.1.call-done.in_hbm = bf16[96,2048]{1,0:T(8,128)(2,1)} async-done(((bf16[1152,2048]{1,0:T(8,128)(2,1)}), bf16[96,2048]{1,0:T(8,128)(2,1)}) %reduce-scatter.2.cloned.1.call-update) | async-done | bytes 393232 | tf_op jit(solution)/shard_map/reduce_scatter | solution.py:204
  151.1 13.0 %split.1 = (bf16[1,32,2048]{2,1,0:T(8,128)(2,1)}, bf16[1,32,2048]{2,1,0:T(8,128)(2,1)}, bf16[1,32,2048]{2,1,0:T(8,128)(2,1)}) custom-call(bf16[96,2048]{1,0:T(8,128)(2,1)} %reduce-scatter.2.cloned.1.call-done.in_hbm), custom_call_target="tpu_custom_call" | custom-call | bytes 393216 | tf_op jit(solution)/shard_map/split/pallas_call | solution.py:220
Async XLA Ops:
  7.2 143.9 %reduce-scatter.2.cloned.1.call-start = ((), (), s32[]{:S(2)}) async-start(), calls=%async_computation.3 | async-start | bytes 5111808 | tf_op jit(solution)/shard_map/reduce_scatter | solution.py:204
  7.2 64.7 %copy-start.5 = (bf16[1,384,2048]{2,1,0:T(8,128)(2,1)S(1)}, bf16[1,384,2048]{2,1,0:T(8,128)(2,1)}, u32[]{:S(2)}) copy-start(bf16[1,384,2048]{2,1,0:T(8,128)(2,1)} %down_hbm.1) | copy-start | bytes 4718596
  9.9 62.1 %copy-start.3 = (bf16[1,2048,384]{2,1,0:T(8,128)(2,1)S(1)}, bf16[1,2048,384]{2,1,0:T(8,128)(2,1)}, u32[]{:S(2)}) copy-start(bf16[1,2048,384]{2,1,0:T(8,128)(2,1)} %gate_ref.3) | copy-start | bytes 4718596
  9.9 62.1 %copy-start.4 = (bf16[1,2048,384]{2,1,0:T(8,128)(2,1)S(1)}, bf16[1,2048,384]{2,1,0:T(8,128)(2,1)}, u32[]{:S(2)}) copy-start(bf16[1,2048,384]{2,1,0:T(8,128)(2,1)} %up_ref.3) | copy-start | bytes 4718596
  82.2 57.5 %copy-start = (bf16[128,2048]{1,0:T(8,128)(2,1)S(1)}, bf16[128,2048]{1,0:T(8,128)(2,1)}, u32[]{:S(2)}) copy-start(bf16[128,2048]{1,0:T(8,128)(2,1)} %grad_ref.1) | copy-start | bytes 1572868
  82.2 57.5 %copy-start.1 = (s32[128,1]{0,1:T(1,128)S(1)}, s32[128,1]{0,1:T(1,128)}, u32[]{:S(2)}) copy-start(s32[128,1]{0,1:T(1,128)} %param.8) | copy-start | bytes 1540
  82.2 57.5 %copy-start.2 = (f32[128,1]{0,1:T(1,128)S(1)}, f32[128,1]{0,1:T(1,128)}, u32[]{:S(2)}) copy-start(f32[128,1]{0,1:T(1,128)} %param.9) | copy-start | bytes 1540
Sparse Core Ops, SparseCore 0:
  77.8 73.2 reduce-scatter.1

commit v3 on v2

--- a/solution.py
+++ b/solution.py
@@ -9,6 +9,7 @@
 
 BF16 = jnp.bfloat16
 F32 = jnp.float32
+COLS = 4
 VMEM = pl.BlockSpec(memory_space=pltpu.VMEM)
 HBM = pl.BlockSpec(memory_space=pltpu.HBM)
 
@@ -75,12 +76,12 @@
     capacity, parts, in_ref, gate_ref, up_ref, down_ref, terms_hbm, factors_hbm,
     terms_ref, factors_ref, sems,
 ):
-    rows = in_ref.shape[0] // 2
-    both = in_ref[...]
-    incoming = dot(pick(rows, capacity, 0), both, 1, 0).astype(BF16)
+    rows, width = in_ref.shape[0] // 2, in_ref.shape[1]
+    both = in_ref[...].reshape(rows // capacity, 2 * capacity, width)
+    incoming = both[:, :capacity].reshape(rows, width)
+    expert_grad = both[:, capacity:].reshape(rows, width)
     pre_gate = dot(incoming, gate_ref[0], 1, 0)
     pre_up = dot(incoming, up_ref[0], 1, 0)
-    expert_grad = dot(pick(rows, capacity, 1), both, 1, 0).astype(BF16)
     sigma = jax.nn.sigmoid(pre_gate)
     activated = pre_gate * sigma
     slope = sigma * (1.0 + pre_gate * (1.0 - sigma))
@@ -91,15 +92,23 @@
     units = hidden.shape[1]
     for k, factor in enumerate((dgate, dup, hidden)):
         factors_ref[:, k * units : (k + 1) * units] = factor
-    stores = [pltpu.make_async_copy(factors_ref, factors_hbm, sems.at[3])]
+    stores = [pltpu.make_async_copy(factors_ref, factors_hbm, sems.at[0])]
     stores[0].start()
+    step = width // COLS
     for k, (factor, operand) in enumerate(
         ((dgate, incoming), (dup, incoming), (hidden, expert_grad))
     ):
-        term = dot(factor, operand, 0, 0).astype(BF16)
-        terms_ref[:, k] = term.reshape(parts, term.shape[0] // parts, term.shape[1])
-        stores.append(pltpu.make_async_copy(terms_ref.at[:, k], terms_hbm.at[:, k], sems.at[k]))
-        stores[-1].start()
+        for h in range(COLS):
+            cols = pl.ds(h * step, step)
+            term = dot(factor, operand[:, h * step : (h + 1) * step], 0, 0).astype(BF16)
+            terms_ref[:, k, :, cols] = term.reshape(parts, units // parts, step)
+            stores.append(
+                pltpu.make_async_copy(
+                    terms_ref.at[:, k, :, cols], terms_hbm.at[:, k, :, cols],
+                    sems.at[len(stores)],
+                )
+            )
+            stores[-1].start()
     for store in stores:
         store.wait()
 
@@ -142,16 +151,20 @@
 
 
 def split_kernel(in_hbm, *refs):
-    outs, sems = refs[:3], refs[3]
+    outs, held, sems = refs[:3], refs[3], refs[4]
     part = in_hbm.shape[0] // 3
-    copies = [
-        pltpu.make_async_copy(in_hbm.at[pl.ds(k * part, part)], out.at[0], sems.at[k])
-        for k, out in enumerate(outs)
+    loads = [
+        pltpu.make_async_copy(in_hbm.at[pl.ds(k * part, part)], held.at[k], sems.at[k])
+        for k in range(3)
     ]
-    for copy in copies:
-        copy.start()
-    for copy in copies:
-        copy.wait()
+    stores = [pltpu.make_async_copy(held.at[k], outs[k].at[0], sems.at[3 + k]) for k in range(3)]
+    for load in loads:
+        load.start()
+    for load, store in zip(loads, stores):
+        load.wait()
+        store.start()
+    for store in stores:
+        store.wait()
 
 
 def call(kernel, out_shape, in_specs, out_specs, scratch, vmem_mib, flops, traffic, name):
@@ -198,7 +211,7 @@
     terms, factors = call(
         functools.partial(terms_kernel, capacity, parts),
         (pltpu.HBM(blocks, BF16), pltpu.HBM((rows, 3 * units), BF16)), [VMEM] * 4, [HBM] * 2,
-        [pltpu.VMEM(blocks, BF16), pltpu.VMEM((rows, 3 * units), BF16), dma((4,))],
+        [pltpu.VMEM(blocks, BF16), pltpu.VMEM((rows, 3 * units), BF16), dma((3 * COLS + 1,))],
         20, 18 * rows * width * units, 10 * width * units + 4 * rows * width, "terms",
     )(incoming, w_gate, w_up, w_down)
     shares = lax.psum_scatter(
@@ -218,7 +231,8 @@
     )(ids, gate_row, out_grad, back)
     share = pltpu.HBM((1, units // parts, width), BF16)
     grads = call(
-        split_kernel, (share,) * 3, [HBM], [HBM] * 3, [dma((3,))], 4, 0, 2 * 3 * units // parts * width, "split"
+        split_kernel, (share,) * 3, [HBM], [HBM] * 3,
+        [pltpu.VMEM((3, units // parts, width), BF16), dma((6,))], 4, 0, 2 * 3 * units // parts * width, "split"
     )(*in_hbm(shares))
     return (layer_out, grad_in, grad_gates.reshape(tok, 1), *grads)
 

time: 171 us -> 159 us (0.930)
  Pallas kernels: 27.7 us -> 15 us
    pallas_call x1, Pallas kernels: 13 us -> 1.73 us  [on_device(): call(split_kernel, (share,) * 3, [HBM], [HBM] * 3, [pltpu.VMEM((3, units...]
where the time goes in v3:
time: 159 us; the launch traced here: 158 us
  blocking collectives  120 us (75%)
  Pallas kernels  15 us (9%)
  between operations  14.1 us (9%)
  waiting for transfers between devices  9.55 us (6%)
    all_to_all x2, blocking collectives, move_rows(): lax.all_to_all(buffer, ('node', 'local'), split_axis=0, concat_axis=0, ti...  120 us
    reduce_scatter x1, waiting for transfers between devices, on_device(): lax.psum_scatter(terms.reshape(3 * units, width), 'dp', scatter_dimension...  9.53 us
    pallas_call x1, Pallas kernels, on_device(): call(functools.partial(returns_kernel, capacity), sds((2 * rows, width),...  4.51 us
    pallas_call x1, Pallas kernels, on_device(): call(functools.partial(terms_kernel, capacity, parts), (pltpu.HBM(blocks,...  4.38 us
  transfers between devices with their start and end apart: 1, of which 1 were waited for; matrix products, arithmetic and copies ran while one was open for 0% of the time, Pallas kernels for 4%

profile of v3, /device:TPU:6, one launch (start us, length us, event | category | flops | bytes accessed | tf_op | source)
XLA Modules:
  0.0 158.3 jit_solution(12180538223376363835)
XLA Ops:
  7.2 0.0 reduce-scatter.2.cloned.1.call-start
  7.2 0.0 copy-start.5
  7.2 2.6 %dispatch.1 = bf16[512,2048]{1,0:T(8,128)(2,1)S(1)} custom-call(s32[1,128]{1,0:T(1,128)} %bitcast.12, f32[1,128]{1,0:T(1,128)} %bitcast.14, bf16[128,2048]{1,0:T(8,128)(2,1)} %tokens_hbm.1, bf16[128,2048]{1,0:T(8,128)(2,1)} %grad_ref.1), custom_call_target="tpu_custom_call" | custom-call | flops 536870912 | bytes 2097152 | tf_op jit(solution)/shard_map/dispatch/pallas_call | solution.py:202
  9.9 0.0 copy-start.3
  9.9 0.0 copy-start.4
  9.9 62.0 %all_to_all.10 = bf16[64,8,2048]{2,1,0:T(8,128)(2,1)S(1)} all-to-all(bf16[64,8,2048]{2,1,0:T(8,128)(2,1)S(1)} %bitcast.9), channel_id=1, replica_groups=mesh['dp'=12,'node'=8,'local'=8] {'node','local'}, dimensions={0} | all-to-all | bytes 4194304 | tf_op jit(solution)/shard_map/all_to_all | solution.py:188
  71.9 0.0 copy-done.5
  71.9 0.0 copy-done.3
  71.9 0.0 copy-done.4
  71.9 4.4 %terms.1 = (bf16[12,3,32,2048]{3,2,1,0:T(8,128)(2,1)}, bf16[256,1152]{1,0:T(8,128)(2,1)}) custom-call(bf16[512,2048]{1,0:T(8,128)(2,1)S(1)} %bitcast.10, bf16[1,2048,384]{2,1,0:T(8,128)(2,1)S(1)} %copy-done.3, bf16[1,2048,384]{2,1,0:T(8,128)(2,1)S(1)} %copy-done.4, bf16[1,384,2048]{2,1,0:T(8,128)(2,1)S(1)} %copy-done.5), custom_call_target="tpu_custom_call" | custom-call | flops 3623878656 | bytes 9961472 | tf_op jit(solution)/shard_map/terms/pallas_call | solution.py:211
  76.3 0.0 reduce-scatter.2.cloned.1.call-update
  76.3 4.5 %returns.1 = bf16[512,2048]{1,0:T(8,128)(2,1)S(1)} custom-call(bf16[256,1152]{1,0:T(8,128)(2,1)} %get-tuple-element.14.factors_hbm, bf16[1,2048,384]{2,1,0:T(8,128)(2,1)S(1)} %copy-done.3, bf16[1,2048,384]{2,1,0:T(8,128)(2,1)S(1)} %copy-done.4, bf16[1,384,2048]{2,1,0:T(8,128)(2,1)} %down_hbm.1), custom_call_target="tpu_custom_call" | custom-call | flops 2013265920 | bytes 6815744 | tf_op jit(solution)/shard_map/returns/pallas_call | solution.py:220
  80.9 0.0 copy-start
  80.9 0.0 copy-start.1
  80.9 0.0 copy-start.2
  80.9 57.5 %all_to_all.11 = bf16[64,8,2048]{2,1,0:T(8,128)(2,1)S(1)} all-to-all(bf16[64,8,2048]{2,1,0:T(8,128)(2,1)S(1)} %bitcast.11), channel_id=1, replica_groups=mesh['dp'=12,'node'=8,'local'=8] {'node','local'}, dimensions={0} | all-to-all | bytes 4194304 | tf_op jit(solution)/shard_map/all_to_all | solution.py:188
  138.4 0.0 copy-done
  138.4 0.0 copy-done.1
  138.4 0.0 copy-done.2
  138.4 1.8 %combine.1 = (bf16[128,2048]{1,0:T(8,128)(2,1)}, bf16[128,2048]{1,0:T(8,128)(2,1)}, f32[1,128]{1,0:T(1,128)}) custom-call(s32[1,128]{1,0:T(1,128)S(1)} %bitcast.13, f32[1,128]{1,0:T(1,128)S(1)} %bitcast.15, bf16[128,2048]{1,0:T(8,128)(2,1)S(1)} %copy-done, bf16[512,2048]{1,0:T(8,128)(2,1)S(1)} %bitcast.8), custom_call_target="tpu_custom_call" | custom-call | flops 536870912 | bytes 2621440 | tf_op jit(solution)/shard_map/combine/pallas_call | solution.py:227
  140.2 9.5 %reduce-scatter.2.cloned.1.call-done.in_hbm = bf16[96,2048]{1,0:T(8,128)(2,1)} async-done(((bf16[1152,2048]{1,0:T(8,128)(2,1)}), bf16[96,2048]{1,0:T(8,128)(2,1)}) %reduce-scatter.2.cloned.1.call-update) | async-done | bytes 393232 | tf_op jit(solution)/shard_map/reduce_scatter | solution.py:217
  149.7 1.7 %split.1 = (bf16[1,32,2048]{2,1,0:T(8,128)(2,1)}, bf16[1,32,2048]{2,1,0:T(8,128)(2,1)}, bf16[1,32,2048]{2,1,0:T(8,128)(2,1)}) custom-call(bf16[96,2048]{1,0:T(8,128)(2,1)} %reduce-scatter.2.cloned.1.call-done.in_hbm), custom_call_target="tpu_custom_call" | custom-call | bytes 393216 | tf_op jit(solution)/shard_map/split/pallas_call | solution.py:233
Async XLA Ops:
  7.2 142.6 %reduce-scatter.2.cloned.1.call-start = ((), (), s32[]{:S(2)}) async-start(), calls=%async_computation.3 | async-start | bytes 5111808 | tf_op jit(solution)/shard_map/reduce_scatter | solution.py:217
  7.2 64.7 %copy-start.5 = (bf16[1,384,2048]{2,1,0:T(8,128)(2,1)S(1)}, bf16[1,384,2048]{2,1,0:T(8,128)(2,1)}, u32[]{:S(2)}) copy-start(bf16[1,384,2048]{2,1,0:T(8,128)(2,1)} %down_hbm.1) | copy-start | bytes 4718596
  9.9 62.1 %copy-start.3 = (bf16[1,2048,384]{2,1,0:T(8,128)(2,1)S(1)}, bf16[1,2048,384]{2,1,0:T(8,128)(2,1)}, u32[]{:S(2)}) copy-start(bf16[1,2048,384]{2,1,0:T(8,128)(2,1)} %gate_ref.3) | copy-start | bytes 4718596
  9.9 62.1 %copy-start.4 = (bf16[1,2048,384]{2,1,0:T(8,128)(2,1)S(1)}, bf16[1,2048,384]{2,1,0:T(8,128)(2,1)}, u32[]{:S(2)}) copy-start(bf16[1,2048,384]{2,1,0:T(8,128)(2,1)} %up_ref.3) | copy-start | bytes 4718596
  80.9 57.5 %copy-start = (bf16[128,2048]{1,0:T(8,128)(2,1)S(1)}, bf16[128,2048]{1,0:T(8,128)(2,1)}, u32[]{:S(2)}) copy-start(bf16[128,2048]{1,0:T(8,128)(2,1)} %grad_ref.1) | copy-start | bytes 1572868
  80.9 57.5 %copy-start.1 = (s32[128,1]{0,1:T(1,128)S(1)}, s32[128,1]{0,1:T(1,128)}, u32[]{:S(2)}) copy-start(s32[128,1]{0,1:T(1,128)} %param.8) | copy-start | bytes 1540
  80.9 57.5 %copy-start.2 = (f32[128,1]{0,1:T(1,128)S(1)}, f32[128,1]{0,1:T(1,128)}, u32[]{:S(2)}) copy-start(f32[128,1]{0,1:T(1,128)} %param.9) | copy-start | bytes 1540
Sparse Core Ops, SparseCore 0:
  76.5 73.2 reduce-scatter.1

commit v4 on v3

--- a/solution.py
+++ b/solution.py
@@ -56,15 +56,14 @@
     loads[0].wait()
     target = slots_of(ids_ref[...], experts, capacity)
     rows = 2 * capacity * experts
-    to_token, to_grad = hot(target, rows), hot(target + capacity, rows)
+    place = jnp.concatenate([hot(target, rows), hot(target + capacity, rows)], axis=1)
     loads[1].wait()
     gates = column_of(gates_ref[...])
     loads[2].wait()
-    out = dot(to_token, tokens_ref[...], 1, 0)
     loads[3].wait()
     scaled = (gates * grad_ref[...].astype(F32)).astype(BF16)
-    out += dot(to_grad, scaled, 1, 0)
-    out_ref[...] = out.astype(BF16)
+    both = jnp.concatenate([tokens_ref[...], scaled], axis=0)
+    out_ref[...] = dot(place, both, 1, 0).astype(BF16)
 
 
 def pick(rows, capacity, kind):

time: 159 us -> 158 us (level)
  no operation moved by 1% of the time
where the time goes in v4:
time: 158 us
  blocking collectives  120 us (76%)
  Pallas kernels  14.5 us (9%)
  between operations  14.1 us (9%)
  waiting for transfers between devices  9.38 us (6%)
    all_to_all x2, blocking collectives, move_rows(): lax.all_to_all(buffer, ('node', 'local'), split_axis=0, concat_axis=0, ti...  120 us
    reduce_scatter x1, waiting for transfers between devices, on_device(): lax.psum_scatter(terms.reshape(3 * units, width), 'dp', scatter_dimension...  9.37 us
    pallas_call x1, Pallas kernels, on_device(): call(functools.partial(returns_kernel, capacity), sds((2 * rows, width),...  4.52 us
    pallas_call x1, Pallas kernels, on_device(): call(functools.partial(terms_kernel, capacity, parts), (pltpu.HBM(blocks,...  4.38 us
  transfers between devices with their start and end apart: 1, of which 1 were waited for; matrix products, arithmetic and copies ran while one was open for 0% of the time, Pallas kernels for 4%

profile of v4, /device:TPU:6, one launch (start us, length us, event | category | flops | bytes accessed | tf_op | source)
XLA Modules:
  0.0 157.6 jit_solution(15747645706686472328)
XLA Ops:
  7.2 0.0 reduce-scatter.2.cloned.1.call-start
  7.2 0.0 copy-start.5
  7.2 2.1 %dispatch.1 = bf16[512,2048]{1,0:T(8,128)(2,1)S(1)} custom-call(s32[1,128]{1,0:T(1,128)} %bitcast.12, f32[1,128]{1,0:T(1,128)} %bitcast.14, bf16[128,2048]{1,0:T(8,128)(2,1)} %tokens_hbm.1, bf16[128,2048]{1,0:T(8,128)(2,1)} %grad_ref.1), custom_call_target="tpu_custom_call" | custom-call | flops 536870912 | bytes 2097152 | tf_op jit(solution)/shard_map/dispatch/pallas_call | solution.py:201
  9.3 0.0 copy-start.3
  9.4 0.0 copy-start.4
  9.4 62.0 %all_to_all.10 = bf16[64,8,2048]{2,1,0:T(8,128)(2,1)S(1)} all-to-all(bf16[64,8,2048]{2,1,0:T(8,128)(2,1)S(1)} %bitcast.9), channel_id=1, replica_groups=mesh['dp'=12,'node'=8,'local'=8] {'node','local'}, dimensions={0} | all-to-all | bytes 4194304 | tf_op jit(solution)/shard_map/all_to_all | solution.py:187
  71.4 0.0 copy-done.5
  71.4 0.0 copy-done.3
  71.4 0.0 copy-done.4
  71.4 4.4 %terms.1 = (bf16[12,3,32,2048]{3,2,1,0:T(8,128)(2,1)}, bf16[256,1152]{1,0:T(8,128)(2,1)}) custom-call(bf16[512,2048]{1,0:T(8,128)(2,1)S(1)} %bitcast.10, bf16[1,2048,384]{2,1,0:T(8,128)(2,1)S(1)} %copy-done.3, bf16[1,2048,384]{2,1,0:T(8,128)(2,1)S(1)} %copy-done.4, bf16[1,384,2048]{2,1,0:T(8,128)(2,1)S(1)} %copy-done.5), custom_call_target="tpu_custom_call" | custom-call | flops 3623878656 | bytes 9961472 | tf_op jit(solution)/shard_map/terms/pallas_call | solution.py:210
  75.8 0.0 reduce-scatter.2.cloned.1.call-update
  75.8 4.5 %returns.1 = bf16[512,2048]{1,0:T(8,128)(2,1)S(1)} custom-call(bf16[256,1152]{1,0:T(8,128)(2,1)} %get-tuple-element.14.factors_hbm, bf16[1,2048,384]{2,1,0:T(8,128)(2,1)S(1)} %copy-done.3, bf16[1,2048,384]{2,1,0:T(8,128)(2,1)S(1)} %copy-done.4, bf16[1,384,2048]{2,1,0:T(8,128)(2,1)} %down_hbm.1), custom_call_target="tpu_custom_call" | custom-call | flops 2013265920 | bytes 6815744 | tf_op jit(solution)/shard_map/returns/pallas_call | solution.py:219
  80.3 0.0 copy-start
  80.4 0.0 copy-start.1
  80.4 0.0 copy-start.2
  80.4 57.5 %all_to_all.11 = bf16[64,8,2048]{2,1,0:T(8,128)(2,1)S(1)} all-to-all(bf16[64,8,2048]{2,1,0:T(8,128)(2,1)S(1)} %bitcast.11), channel_id=1, replica_groups=mesh['dp'=12,'node'=8,'local'=8] {'node','local'}, dimensions={0} | all-to-all | bytes 4194304 | tf_op jit(solution)/shard_map/all_to_all | solution.py:187
  137.9 0.0 copy-done
  137.9 0.0 copy-done.1
  137.9 0.0 copy-done.2
  137.9 1.8 %combine.1 = (bf16[128,2048]{1,0:T(8,128)(2,1)}, bf16[128,2048]{1,0:T(8,128)(2,1)}, f32[1,128]{1,0:T(1,128)}) custom-call(s32[1,128]{1,0:T(1,128)S(1)} %bitcast.13, f32[1,128]{1,0:T(1,128)S(1)} %bitcast.15, bf16[128,2048]{1,0:T(8,128)(2,1)S(1)} %copy-done, bf16[512,2048]{1,0:T(8,128)(2,1)S(1)} %bitcast.8), custom_call_target="tpu_custom_call" | custom-call | flops 536870912 | bytes 2621440 | tf_op jit(solution)/shard_map/combine/pallas_call | solution.py:226
  139.7 9.4 %reduce-scatter.2.cloned.1.call-done.in_hbm = bf16[96,2048]{1,0:T(8,128)(2,1)} async-done(((bf16[1152,2048]{1,0:T(8,128)(2,1)}), bf16[96,2048]{1,0:T(8,128)(2,1)}) %reduce-scatter.2.cloned.1.call-update) | async-done | bytes 393232 | tf_op jit(solution)/shard_map/reduce_scatter | solution.py:216
  149.0 1.7 %split.1 = (bf16[1,32,2048]{2,1,0:T(8,128)(2,1)}, bf16[1,32,2048]{2,1,0:T(8,128)(2,1)}, bf16[1,32,2048]{2,1,0:T(8,128)(2,1)}) custom-call(bf16[96,2048]{1,0:T(8,128)(2,1)} %reduce-scatter.2.cloned.1.call-done.in_hbm), custom_call_target="tpu_custom_call" | custom-call | bytes 393216 | tf_op jit(solution)/shard_map/split/pallas_call | solution.py:232
Async XLA Ops:
  7.2 141.9 %reduce-scatter.2.cloned.1.call-start = ((), (), s32[]{:S(2)}) async-start(), calls=%async_computation.3 | async-start | bytes 5111808 | tf_op jit(solution)/shard_map/reduce_scatter | solution.py:216
  7.2 64.2 %copy-start.5 = (bf16[1,384,2048]{2,1,0:T(8,128)(2,1)S(1)}, bf16[1,384,2048]{2,1,0:T(8,128)(2,1)}, u32[]{:S(2)}) copy-start(bf16[1,384,2048]{2,1,0:T(8,128)(2,1)} %down_hbm.1) | copy-start | bytes 4718596
  9.3 62.1 %copy-start.3 = (bf16[1,2048,384]{2,1,0:T(8,128)(2,1)S(1)}, bf16[1,2048,384]{2,1,0:T(8,128)(2,1)}, u32[]{:S(2)}) copy-start(bf16[1,2048,384]{2,1,0:T(8,128)(2,1)} %gate_ref.3) | copy-start | bytes 4718596
  9.4 62.1 %copy-start.4 = (bf16[1,2048,384]{2,1,0:T(8,128)(2,1)S(1)}, bf16[1,2048,384]{2,1,0:T(8,128)(2,1)}, u32[]{:S(2)}) copy-start(bf16[1,2048,384]{2,1,0:T(8,128)(2,1)} %up_ref.3) | copy-start | bytes 4718596
  80.3 57.5 %copy-start = (bf16[128,2048]{1,0:T(8,128)(2,1)S(1)}, bf16[128,2048]{1,0:T(8,128)(2,1)}, u32[]{:S(2)}) copy-start(bf16[128,2048]{1,0:T(8,128)(2,1)} %grad_ref.1) | copy-start | bytes 1572868
  80.4 57.5 %copy-start.1 = (s32[128,1]{0,1:T(1,128)S(1)}, s32[128,1]{0,1:T(1,128)}, u32[]{:S(2)}) copy-start(s32[128,1]{0,1:T(1,128)} %param.8) | copy-start | bytes 1540
  80.4 57.5 %copy-start.2 = (f32[128,1]{0,1:T(1,128)S(1)}, f32[128,1]{0,1:T(1,128)}, u32[]{:S(2)}) copy-start(f32[128,1]{0,1:T(1,128)} %param.9) | copy-start | bytes 1540
Sparse Core Ops, SparseCore 0:
  75.9 73.0 reduce-scatter.1

commit v5 on v4

--- a/solution.py
+++ b/solution.py
@@ -64,11 +64,6 @@
     scaled = (gates * grad_ref[...].astype(F32)).astype(BF16)
     both = jnp.concatenate([tokens_ref[...], scaled], axis=0)
     out_ref[...] = dot(place, both, 1, 0).astype(BF16)
-
-
-def pick(rows, capacity, kind):
-    at, of = iota((rows, 2 * rows), 0), iota((rows, 2 * rows), 1)
-    return (of == at + (at // capacity + kind) * capacity).astype(F32).astype(BF16)
 
 
 def terms_kernel(
@@ -121,16 +116,15 @@
     )
     for load in loads:
         load.start()
-    for load in loads:
-        load.wait()
-    rows, units = factors_ref.shape[0], gate_ref.shape[2]
+    rows, units, width = factors_ref.shape[0], gate_ref.shape[2], out_ref.shape[1]
+    loads[0].wait()
     dgate, dup, hidden = (factors_ref[:, k * units : (k + 1) * units] for k in range(3))
-    back = dot(hidden, down_ref[0], 1, 0).astype(BF16)
-    grad = (
-        dot(dgate, gate_ref[0], 1, 1) + dot(dup, up_ref[0], 1, 1)
-    ).astype(BF16)
-    out = dot(pick(rows, capacity, 0), back, 0, 0) + dot(pick(rows, capacity, 1), grad, 0, 0)
-    out_ref[...] = out.astype(BF16)
+    grad = dot(dgate, gate_ref[0], 1, 1) + dot(dup, up_ref[0], 1, 1)
+    loads[1].wait()
+    back = dot(hidden, down_ref[0], 1, 0)
+    groups = (rows // capacity, capacity, width)
+    both = [x.astype(BF16).reshape(groups) for x in (back, grad)]
+    out_ref[...] = jnp.concatenate(both, axis=1).reshape(2 * rows, width)
 
 
 def combine_kernel(

time: 158 us -> 158 us (level)
  transfers between devices with their start and end apart: 1 -> 1, of which waited for: 1 -> 1; matrix products, arithmetic and copies ran while one was open for 0% -> 0% of each run, Pallas kernels for 4% -> 3%
where the time goes in v5:
time: 158 us
  blocking collectives  120 us (76%)
  between operations  14.1 us (9%)
  Pallas kernels  13.4 us (8%)
  waiting for transfers between devices  10.4 us (7%)
    all_to_all x2, blocking collectives, move_rows(): lax.all_to_all(buffer, ('node', 'local'), split_axis=0, concat_axis=0, ti...  120 us
    reduce_scatter x1, waiting for transfers between devices, on_device(): lax.psum_scatter(terms.reshape(3 * units, width), 'dp', scatter_dimension...  10.4 us
    pallas_call x1, Pallas kernels, on_device(): call(functools.partial(terms_kernel, capacity, parts), (pltpu.HBM(blocks,...  4.38 us
    pallas_call x1, Pallas kernels, on_device(): call(functools.partial(returns_kernel, capacity), sds((2 * rows, width),...  3.45 us
  transfers between devices with their start and end apart: 1, of which 1 were waited for; matrix products, arithmetic and copies ran while one was open for 0% of the time, Pallas kernels for 3%

profile of v5, /device:TPU:6, one launch (start us, length us, event | category | flops | bytes accessed | tf_op | source)
XLA Modules:
  0.0 157.6 jit_solution(3519380444591651422)
XLA Ops:
  7.2 0.0 reduce-scatter.2.cloned.1.call-start
  7.2 0.0 copy-start.5
  7.2 2.1 %dispatch.1 = bf16[512,2048]{1,0:T(8,128)(2,1)S(1)} custom-call(s32[1,128]{1,0:T(1,128)} %bitcast.12, f32[1,128]{1,0:T(1,128)} %bitcast.14, bf16[128,2048]{1,0:T(8,128)(2,1)} %tokens_hbm.1, bf16[128,2048]{1,0:T(8,128)(2,1)} %grad_ref.1), custom_call_target="tpu_custom_call" | custom-call | flops 536870912 | bytes 2097152 | tf_op jit(solution)/shard_map/dispatch/pallas_call | solution.py:195
  9.3 0.0 copy-start.3
  9.4 0.0 copy-start.4
  9.4 62.0 %all_to_all.10 = bf16[64,8,2048]{2,1,0:T(8,128)(2,1)S(1)} all-to-all(bf16[64,8,2048]{2,1,0:T(8,128)(2,1)S(1)} %bitcast.9), channel_id=1, replica_groups=mesh['dp'=12,'node'=8,'local'=8] {'node','local'}, dimensions={0} | all-to-all | bytes 4194304 | tf_op jit(solution)/shard_map/all_to_all | solution.py:181
  71.4 0.0 copy-done.5
  71.4 0.0 copy-done.3
  71.4 0.0 copy-done.4
  71.4 4.4 %terms.1 = (bf16[12,3,32,2048]{3,2,1,0:T(8,128)(2,1)}, bf16[256,1152]{1,0:T(8,128)(2,1)}) custom-call(bf16[512,2048]{1,0:T(8,128)(2,1)S(1)} %bitcast.10, bf16[1,2048,384]{2,1,0:T(8,128)(2,1)S(1)} %copy-done.3, bf16[1,2048,384]{2,1,0:T(8,128)(2,1)S(1)} %copy-done.4, bf16[1,384,2048]{2,1,0:T(8,128)(2,1)S(1)} %copy-done.5), custom_call_target="tpu_custom_call" | custom-call | flops 3623878656 | bytes 9961472 | tf_op jit(solution)/shard_map/terms/pallas_call | solution.py:204
  75.8 0.0 reduce-scatter.2.cloned.1.call-update
  75.8 3.5 %returns.1 = bf16[512,2048]{1,0:T(8,128)(2,1)S(1)} custom-call(bf16[256,1152]{1,0:T(8,128)(2,1)} %get-tuple-element.14.factors_hbm, bf16[1,2048,384]{2,1,0:T(8,128)(2,1)S(1)} %copy-done.3, bf16[1,2048,384]{2,1,0:T(8,128)(2,1)S(1)} %copy-done.4, bf16[1,384,2048]{2,1,0:T(8,128)(2,1)} %down_hbm.1), custom_call_target="tpu_custom_call" | custom-call | flops 2013265920 | bytes 6815744 | tf_op jit(solution)/shard_map/returns/pallas_call | solution.py:213
  79.3 0.0 copy-start
  79.3 0.0 copy-start.1
  79.3 0.0 copy-start.2
  79.3 57.5 %all_to_all.11 = bf16[64,8,2048]{2,1,0:T(8,128)(2,1)S(1)} all-to-all(bf16[64,8,2048]{2,1,0:T(8,128)(2,1)S(1)} %bitcast.11), channel_id=1, replica_groups=mesh['dp'=12,'node'=8,'local'=8] {'node','local'}, dimensions={0} | all-to-all | bytes 4194304 | tf_op jit(solution)/shard_map/all_to_all | solution.py:181
  136.8 0.0 copy-done
  136.8 0.0 copy-done.1
  136.8 0.0 copy-done.2
  136.8 1.8 %combine.1 = (bf16[128,2048]{1,0:T(8,128)(2,1)}, bf16[128,2048]{1,0:T(8,128)(2,1)}, f32[1,128]{1,0:T(1,128)}) custom-call(s32[1,128]{1,0:T(1,128)S(1)} %bitcast.13, f32[1,128]{1,0:T(1,128)S(1)} %bitcast.15, bf16[128,2048]{1,0:T(8,128)(2,1)S(1)} %copy-done, bf16[512,2048]{1,0:T(8,128)(2,1)S(1)} %bitcast.8), custom_call_target="tpu_custom_call" | custom-call | flops 536870912 | bytes 2621440 | tf_op jit(solution)/shard_map/combine/pallas_call | solution.py:220
  138.6 10.4 %reduce-scatter.2.cloned.1.call-done.in_hbm = bf16[96,2048]{1,0:T(8,128)(2,1)} async-done(((bf16[1152,2048]{1,0:T(8,128)(2,1)}), bf16[96,2048]{1,0:T(8,128)(2,1)}) %reduce-scatter.2.cloned.1.call-update) | async-done | bytes 393232 | tf_op jit(solution)/shard_map/reduce_scatter | solution.py:210
  149.0 1.7 %split.1 = (bf16[1,32,2048]{2,1,0:T(8,128)(2,1)}, bf16[1,32,2048]{2,1,0:T(8,128)(2,1)}, bf16[1,32,2048]{2,1,0:T(8,128)(2,1)}) custom-call(bf16[96,2048]{1,0:T(8,128)(2,1)} %reduce-scatter.2.cloned.1.call-done.in_hbm), custom_call_target="tpu_custom_call" | custom-call | bytes 393216 | tf_op jit(solution)/shard_map/split/pallas_call | solution.py:226
Async XLA Ops:
  7.2 141.9 %reduce-scatter.2.cloned.1.call-start = ((), (), s32[]{:S(2)}) async-start(), calls=%async_computation.3 | async-start | bytes 5111808 | tf_op jit(solution)/shard_map/reduce_scatter | solution.py:210
  7.2 64.2 %copy-start.5 = (bf16[1,384,2048]{2,1,0:T(8,128)(2,1)S(1)}, bf16[1,384,2048]{2,1,0:T(8,128)(2,1)}, u32[]{:S(2)}) copy-start(bf16[1,384,2048]{2,1,0:T(8,128)(2,1)} %down_hbm.1) | copy-start | bytes 4718596
  9.3 62.1 %copy-start.3 = (bf16[1,2048,384]{2,1,0:T(8,128)(2,1)S(1)}, bf16[1,2048,384]{2,1,0:T(8,128)(2,1)}, u32[]{:S(2)}) copy-start(bf16[1,2048,384]{2,1,0:T(8,128)(2,1)} %gate_ref.3) | copy-start | bytes 4718596
  9.4 62.1 %copy-start.4 = (bf16[1,2048,384]{2,1,0:T(8,128)(2,1)S(1)}, bf16[1,2048,384]{2,1,0:T(8,128)(2,1)}, u32[]{:S(2)}) copy-start(bf16[1,2048,384]{2,1,0:T(8,128)(2,1)} %up_ref.3) | copy-start | bytes 4718596
  79.3 57.5 %copy-start = (bf16[128,2048]{1,0:T(8,128)(2,1)S(1)}, bf16[128,2048]{1,0:T(8,128)(2,1)}, u32[]{:S(2)}) copy-start(bf16[128,2048]{1,0:T(8,128)(2,1)} %grad_ref.1) | copy-start | bytes 1572868
  79.3 57.5 %copy-start.1 = (s32[128,1]{0,1:T(1,128)S(1)}, s32[128,1]{0,1:T(1,128)}, u32[]{:S(2)}) copy-start(s32[128,1]{0,1:T(1,128)} %param.8) | copy-start | bytes 1540
  79.3 57.5 %copy-start.2 = (f32[128,1]{0,1:T(1,128)S(1)}, f32[128,1]{0,1:T(1,128)}, u32[]{:S(2)}) copy-start(f32[128,1]{0,1:T(1,128)} %param.9) | copy-start | bytes 1540
Sparse Core Ops, SparseCore 0:
  75.9 73.0 reduce-scatter.1

commit v6 on v5

--- a/solution.py
+++ b/solution.py
@@ -67,7 +67,7 @@
 
 
 def terms_kernel(
-    capacity, parts, in_ref, gate_ref, up_ref, down_ref, terms_hbm, factors_hbm,
+    capacity, in_ref, gate_ref, up_ref, down_ref, terms_hbm, factors_hbm,
     terms_ref, factors_ref, sems,
 ):
     rows, width = in_ref.shape[0] // 2, in_ref.shape[1]
@@ -95,10 +95,10 @@
         for h in range(COLS):
             cols = pl.ds(h * step, step)
             term = dot(factor, operand[:, h * step : (h + 1) * step], 0, 0).astype(BF16)
-            terms_ref[:, k, :, cols] = term.reshape(parts, units // parts, step)
+            terms_ref[k, :, cols] = term
             stores.append(
                 pltpu.make_async_copy(
-                    terms_ref.at[:, k, :, cols], terms_hbm.at[:, k, :, cols],
+                    terms_ref.at[k, :, cols], terms_hbm.at[k, :, cols],
                     sems.at[len(stores)],
                 )
             )
@@ -145,9 +145,8 @@
 
 def split_kernel(in_hbm, *refs):
     outs, held, sems = refs[:3], refs[3], refs[4]
-    part = in_hbm.shape[0] // 3
     loads = [
-        pltpu.make_async_copy(in_hbm.at[pl.ds(k * part, part)], held.at[k], sems.at[k])
+        pltpu.make_async_copy(in_hbm.at[k], held.at[k], sems.at[k])
         for k in range(3)
     ]
     stores = [pltpu.make_async_copy(held.at[k], outs[k].at[0], sems.at[3 + k]) for k in range(3)]
@@ -200,16 +199,14 @@
         12, 8 * rows * tok * width, 8 * tok * width, "dispatch",
     )(*in_hbm(ids, gate_row, tokens, out_grad))
     incoming = move_rows(outgoing.reshape(experts, 2 * capacity, width)).reshape(2 * rows, width)
-    blocks = (parts, 3, units // parts, width)
+    blocks = (3, units, width)
     terms, factors = call(
-        functools.partial(terms_kernel, capacity, parts),
+        functools.partial(terms_kernel, capacity),
         (pltpu.HBM(blocks, BF16), pltpu.HBM((rows, 3 * units), BF16)), [VMEM] * 4, [HBM] * 2,
         [pltpu.VMEM(blocks, BF16), pltpu.VMEM((rows, 3 * units), BF16), dma((3 * COLS + 1,))],
         20, 18 * rows * width * units, 10 * width * units + 4 * rows * width, "terms",
     )(incoming, w_gate, w_up, w_down)
-    shares = lax.psum_scatter(
-        terms.reshape(3 * units, width), "dp", scatter_dimension=0, tiled=True
-    )
+    shares = lax.psum_scatter(terms, "dp", scatter_dimension=1, tiled=True)
     back = call(
         functools.partial(returns_kernel, capacity),
         sds((2 * rows, width), BF16), [HBM, VMEM, VMEM, HBM], VMEM,

time: 158 us -> 158 us (level)
  no operation moved by 1% of the time
where the time goes in v6:
time: 158 us
  blocking collectives  120 us (76%)
  between operations  14.1 us (9%)
  Pallas kernels  13.4 us (8%)
  waiting for transfers between devices  10.4 us (7%)
    all_to_all x2, blocking collectives, move_rows(): lax.all_to_all(buffer, ('node', 'local'), split_axis=0, concat_axis=0, ti...  120 us
    reduce_scatter x1, waiting for transfers between devices, on_device(): shares = lax.psum_scatter(terms, 'dp', scatter_dimension=1, tiled=True)  10.4 us
    pallas_call x1, Pallas kernels, on_device(): call(functools.partial(terms_kernel, capacity), (pltpu.HBM(blocks, BF16),...  4.35 us
    pallas_call x1, Pallas kernels, on_device(): call(functools.partial(returns_kernel, capacity), sds((2 * rows, width),...  3.45 us
  transfers between devices with their start and end apart: 1, of which 1 were waited for; matrix products, arithmetic and copies ran while one was open for 0% of the time, Pallas kernels for 3%

profile of v6, /device:TPU:6, one launch (start us, length us, event | category | flops | bytes accessed | tf_op | source)
XLA Modules:
  0.0 157.6 jit_solution(2848493520611443747)
XLA Ops:
  7.2 0.0 reduce-scatter.2.cloned.1.call-start
  7.2 0.0 copy-start.5
  7.2 2.1 %dispatch.1 = bf16[512,2048]{1,0:T(8,128)(2,1)S(1)} custom-call(s32[1,128]{1,0:T(1,128)} %bitcast.11, f32[1,128]{1,0:T(1,128)} %bitcast.13, bf16[128,2048]{1,0:T(8,128)(2,1)} %tokens_hbm.1, bf16[128,2048]{1,0:T(8,128)(2,1)} %grad_ref.1), custom_call_target="tpu_custom_call" | custom-call | flops 536870912 | bytes 2097152 | tf_op jit(solution)/shard_map/dispatch/pallas_call | solution.py:194
  9.3 0.0 copy-start.3
  9.4 0.0 copy-start.4
  9.4 62.0 %all_to_all.10 = bf16[64,8,2048]{2,1,0:T(8,128)(2,1)S(1)} all-to-all(bf16[64,8,2048]{2,1,0:T(8,128)(2,1)S(1)} %bitcast.8), channel_id=1, replica_groups=mesh['dp'=12,'node'=8,'local'=8] {'node','local'}, dimensions={0} | all-to-all | bytes 4194304 | tf_op jit(solution)/shard_map/all_to_all | solution.py:180
  71.4 0.0 copy-done.5
  71.4 0.0 copy-done.3
  71.4 0.0 copy-done.4
  71.4 4.4 %terms.1 = (bf16[3,384,2048]{2,1,0:T(8,128)(2,1)}, bf16[256,1152]{1,0:T(8,128)(2,1)}) custom-call(bf16[512,2048]{1,0:T(8,128)(2,1)S(1)} %bitcast.9, bf16[1,2048,384]{2,1,0:T(8,128)(2,1)S(1)} %copy-done.3, bf16[1,2048,384]{2,1,0:T(8,128)(2,1)S(1)} %copy-done.4, bf16[1,384,2048]{2,1,0:T(8,128)(2,1)S(1)} %copy-done.5), custom_call_target="tpu_custom_call" | custom-call | flops 3623878656 | bytes 9961472 | tf_op jit(solution)/shard_map/terms/pallas_call | solution.py:203
  75.8 0.0 reduce-scatter.2.cloned.1.call-update
  75.8 3.5 %returns.1 = bf16[512,2048]{1,0:T(8,128)(2,1)S(1)} custom-call(bf16[256,1152]{1,0:T(8,128)(2,1)} %get-tuple-element.14.factors_hbm, bf16[1,2048,384]{2,1,0:T(8,128)(2,1)S(1)} %copy-done.3, bf16[1,2048,384]{2,1,0:T(8,128)(2,1)S(1)} %copy-done.4, bf16[1,384,2048]{2,1,0:T(8,128)(2,1)} %down_hbm.1), custom_call_target="tpu_custom_call" | custom-call | flops 2013265920 | bytes 6815744 | tf_op jit(solution)/shard_map/returns/pallas_call | solution.py:210
  79.3 0.0 copy-start
  79.3 0.0 copy-start.1
  79.3 0.0 copy-start.2
  79.3 57.5 %all_to_all.11 = bf16[64,8,2048]{2,1,0:T(8,128)(2,1)S(1)} all-to-all(bf16[64,8,2048]{2,1,0:T(8,128)(2,1)S(1)} %bitcast.10), channel_id=1, replica_groups=mesh['dp'=12,'node'=8,'local'=8] {'node','local'}, dimensions={0} | all-to-all | bytes 4194304 | tf_op jit(solution)/shard_map/all_to_all | solution.py:180
  136.8 0.0 copy-done
  136.8 0.0 copy-done.1
  136.8 0.0 copy-done.2
  136.8 1.8 %combine.1 = (bf16[128,2048]{1,0:T(8,128)(2,1)}, bf16[128,2048]{1,0:T(8,128)(2,1)}, f32[1,128]{1,0:T(1,128)}) custom-call(s32[1,128]{1,0:T(1,128)S(1)} %bitcast.12, f32[1,128]{1,0:T(1,128)S(1)} %bitcast.14, bf16[128,2048]{1,0:T(8,128)(2,1)S(1)} %copy-done, bf16[512,2048]{1,0:T(8,128)(2,1)S(1)} %bitcast.7), custom_call_target="tpu_custom_call" | custom-call | flops 536870912 | bytes 2621440 | tf_op jit(solution)/shard_map/combine/pallas_call | solution.py:217
  138.6 10.4 %reduce-scatter.2.cloned.1.call-done.in_hbm = bf16[3,32,2048]{2,1,0:T(8,128)(2,1)} async-done(((bf16[3,384,2048]{2,1,0:T(8,128)(2,1)}), bf16[3,32,2048]{2,1,0:T(8,128)(2,1)}) %reduce-scatter.2.cloned.1.call-update) | async-done | bytes 393232 | tf_op jit(solution)/shard_map/reduce_scatter | solution.py:209
  149.0 1.7 %split.1 = (bf16[1,32,2048]{2,1,0:T(8,128)(2,1)}, bf16[1,32,2048]{2,1,0:T(8,128)(2,1)}, bf16[1,32,2048]{2,1,0:T(8,128)(2,1)}) custom-call(bf16[3,32,2048]{2,1,0:T(8,128)(2,1)} %reduce-scatter.2.cloned.1.call-done.in_hbm), custom_call_target="tpu_custom_call" | custom-call | bytes 393216 | tf_op jit(solution)/shard_map/split/pallas_call | solution.py:223
Async XLA Ops:
  7.2 141.8 %reduce-scatter.2.cloned.1.call-start = ((), (), s32[]{:S(2)}) async-start(), calls=%async_computation.3 | async-start | bytes 5111808 | tf_op jit(solution)/shard_map/reduce_scatter | solution.py:209
  7.2 64.2 %copy-start.5 = (bf16[1,384,2048]{2,1,0:T(8,128)(2,1)S(1)}, bf16[1,384,2048]{2,1,0:T(8,128)(2,1)}, u32[]{:S(2)}) copy-start(bf16[1,384,2048]{2,1,0:T(8,128)(2,1)} %down_hbm.1) | copy-start | bytes 4718596
  9.3 62.1 %copy-start.3 = (bf16[1,2048,384]{2,1,0:T(8,128)(2,1)S(1)}, bf16[1,2048,384]{2,1,0:T(8,128)(2,1)}, u32[]{:S(2)}) copy-start(bf16[1,2048,384]{2,1,0:T(8,128)(2,1)} %gate_ref.3) | copy-start | bytes 4718596
  9.4 62.1 %copy-start.4 = (bf16[1,2048,384]{2,1,0:T(8,128)(2,1)S(1)}, bf16[1,2048,384]{2,1,0:T(8,128)(2,1)}, u32[]{:S(2)}) copy-start(bf16[1,2048,384]{2,1,0:T(8,128)(2,1)} %up_ref.3) | copy-start | bytes 4718596
  79.3 57.5 %copy-start = (bf16[128,2048]{1,0:T(8,128)(2,1)S(1)}, bf16[128,2048]{1,0:T(8,128)(2,1)}, u32[]{:S(2)}) copy-start(bf16[128,2048]{1,0:T(8,128)(2,1)} %grad_ref.1) | copy-start | bytes 1572868
  79.3 57.5 %copy-start.1 = (s32[128,1]{0,1:T(1,128)S(1)}, s32[128,1]{0,1:T(1,128)}, u32[]{:S(2)}) copy-start(s32[128,1]{0,1:T(1,128)} %param.8) | copy-start | bytes 1540
  79.3 57.5 %copy-start.2 = (f32[128,1]{0,1:T(1,128)S(1)}, f32[128,1]{0,1:T(1,128)}, u32[]{:S(2)}) copy-start(f32[128,1]{0,1:T(1,128)} %param.9) | copy-start | bytes 1540
Sparse Core Ops, SparseCore 0:
  75.9 73.0 reduce-scatter.1
